TPU v7x, 32 devices: a whole 2x2x4 slice. The times are simulated.
32 devices in a mesh: band: 4 (over y, core), tile: 8 (over z, x).
Axes of the slice: x: 2, y: 2, z: 4, core: 2. Of those that a mesh axis runs over, the one named last changes fastest.
Arguments:
- sketch: float32 [8, 4, 48, 128, 128], P(None, 'band', 'tile'), may hold values from -6 to 6
- diag_coef: float32 [4, 48, 128], P('band', 'tile'), may hold values from 1 to 2
- couple: float32 [4, 48, 128], P('band', 'tile'), may hold values from 0.3 to 0.8
- kernel: bfloat16 [8, 512, 4, 48, 128], P(None, None, 'band', 'tile'), may hold values from -0.013671875 to 0.013671875
- noise_prec: float32 [8, 512], replicated, may hold values from 0.5 to 4
Outputs:
- hessian_sketch: float32 [8, 4, 48, 128, 128], P(None, 'band', 'tile')
All inputs are finite; a program needn't handle non-finite values.
Results may differ from a plain program's by a relative error of at most 0.0041.
Values may be sent and summed in bfloat16 or wider, within the bound.
No kernel may reach another device: no remote copies, remote signals or barrier semaphores. Data moves between devices by JAX's collectives and lax.ppermute only.
A program may use at most 128 MiB of HBM per device.

v0:
```python
import functools

import jax
import jax.numpy as jnp
from jax import lax
from jax.experimental import pallas as pl
from jax.experimental.pallas import tpu as pltpu
from jax.sharding import Mesh
from jax.sharding import PartitionSpec as P

MIB = 1 << 20
HALO = 2
VMEM = pl.BlockSpec(memory_space=pltpu.VMEM)
SMEM = pl.BlockSpec(memory_space=pltpu.SMEM)
HBM = pl.BlockSpec(memory_space=pltpu.HBM)


def call(kernel, name, out_shape, in_specs, out_specs, scratch, moved, grid=(), aliases={}, limit=16):
    return pl.pallas_call(
        kernel,
        grid=grid,
        out_shape=out_shape,
        in_specs=in_specs,
        out_specs=out_specs,
        scratch_shapes=scratch,
        input_output_aliases=aliases,
        compiler_params=pltpu.CompilerParams(vmem_limit_bytes=limit * MIB),
        cost_estimate=pl.CostEstimate(flops=0, bytes_accessed=moved * MIB, transcendentals=0),
        name=name,
    )


def f32(*shape):
    return jax.ShapeDtypeStruct(shape, jnp.float32)


def bf16(*shape):
    return jax.ShapeDtypeStruct(shape, jnp.bfloat16)


def edge_rows(rows):
    return [*range(HALO), *range(rows - HALO, rows)]


def beside(w):
    cols = w.shape[0]
    at = lax.broadcasted_iota(jnp.int32, w.shape, 0)
    before = jnp.where(at == 0, 0.0, pltpu.roll(w, 1, 0))
    after = jnp.where(at == cols - 1, 0.0, pltpu.roll(w, cols - 1, 0))
    return before + after


def spread(own, halos, line, wide):
    rows, cols = own[0].shape
    for which in range(2):
        line[...] = jnp.zeros(line.shape, line.dtype)
        for side, halo in enumerate(halos):
            at = side * (HALO + rows)
            line[at : at + HALO, :] = halo[which]
        line[HALO : HALO + rows, :] = own[which][...]
        turned = line[...].T
        for row in range(rows + 2 * HALO):
            wide[which, row] = jnp.broadcast_to(turned[:, row : row + 1], wide.shape[2:])


def mix_coefs(wide, mix):
    total = wide.shape[1]
    for side in range(2):
        far, near, edge, inner = (row if side == 0 else total - 1 - row for row in range(4))
        square = wide[1, edge] * wide[1, edge]
        mix[side, 0] = wide[1, near]
        mix[side, 1] = wide[1, far]
        mix[side, 2] = wide[1, near] * wide[0, near]
        mix[side, 3] = wide[1, near] * wide[1, near]
        mix[side, 4] = -square
        mix[side, 5] = -wide[0, edge] * wide[1, edge]
        mix[side, 6] = wide[1, edge]
        mix[side, 7] = wide[1, inner] * square


def coef_scratch(rows, cols, width):
    return [pltpu.VMEM((cols, cols), jnp.float32), pltpu.VMEM((2, rows, cols, width), jnp.float32)]


def one_sweep(values, scaled, wide, row):
    around = beside(scaled[row])
    if row > 0:
        around = around + scaled[row - 1]
    if row + 1 < len(scaled):
        around = around + scaled[row + 1]
    return wide[0, row + HALO] * values[row] - wide[1, row + HALO] * around


def own_sweeps(load, wide, rows, store):
    values, scaled, first, second = ([None] * rows for _ in range(4))
    for row in range(rows + 2):
        if row < rows:
            values[row] = load(row)
            scaled[row] = wide[1, row + HALO] * values[row]
        if 0 < row <= rows:
            first[row - 1] = one_sweep(values, scaled, wide, row - 1)
            second[row - 1] = wide[1, row - 1 + HALO] * first[row - 1]
        if row > 1:
            store(row - 2, one_sweep(first, second, wide, row - 2), scaled)


def halo_part(message, at, edge_scaled, mix, side):
    cols = edge_scaled.shape[0]
    far_row, near_row = (0, 1) if side == 0 else (1, 0)

    def take(row):
        start = pl.multiple_of(at + row * cols, cols)
        return message[pl.ds(start, cols), :].astype(jnp.float32)

    near = take(near_row)
    scaled = mix[side, 0] * near
    around = mix[side, 1] * take(far_row) + edge_scaled + beside(scaled)
    near_second = mix[side, 2] * near - mix[side, 3] * around
    second = mix[side, 4] * scaled
    on_edge = mix[side, 5] * scaled - mix[side, 6] * (near_second + beside(second))
    return on_edge, mix[side, 7] * scaled


def spots_of(side):
    return (0, 1) if side == 0 else (2 * HALO - 1, 2 * HALO - 2)


def pack_kernel(first, field, _, out, edges, packed, arrived, left):
    steps, rows, cols, width = field.shape
    strip = HALO * cols
    coming, going = [], []
    for step in range(steps):
        source = field.at[step, pl.ds(first, HALO)]
        coming.append(pltpu.make_async_copy(source, edges.at[step], arrived.at[step]))
        coming[step].start()
        going.append(pltpu.make_async_copy(packed.at[step], out.at[pl.ds(step * strip, strip)], left.at[step]))
    for step in range(steps):
        coming[step].wait()
        packed[step] = edges[step].reshape(strip, width).astype(packed.dtype)
        going[step].start()
    for copy in going:
        copy.wait()


def pack(first, field, after):
    steps, rows, cols, width = field.shape
    strip = HALO * cols
    return call(
        functools.partial(pack_kernel, first),
        "pack",
        bf16(steps * strip, width),
        [HBM] * 2,
        HBM,
        [
            pltpu.VMEM((steps, HALO, cols, width), jnp.float32),
            pltpu.VMEM((steps, strip, width), jnp.bfloat16),
            pltpu.SemaphoreType.DMA((steps,)),
            pltpu.SemaphoreType.DMA((steps,)),
        ],
        3,
        limit=62,
    )(field, after)


def before_kernel(field, diag, couple, kern, _, edges, scaled, data, turned, outward, line, wide, pairs):
    steps, rows, cols, width = field.shape
    inner = rows - 2 * HALO
    listed = edge_rows(rows)
    spread((diag, couple), (), line, wide)
    pairs[0, :, 0:width] = jnp.zeros((inner * cols, width), pairs.dtype)

    @pl.loop(0, steps)
    def _(step):
        def store(row, value, weighted):
            if row in listed:
                edges[step, listed.index(row)] = value
            else:
                at = (row - HALO) * cols
                rounded = value.astype(pairs.dtype)
                pairs[step, at : at + cols, width : 2 * width] = rounded
                pairs[step + 1, at : at + cols, 0:width] = rounded
            if row == 0:
                scaled[step, 0] = weighted[0]
            if row == rows - 1:
                scaled[step, 1] = weighted[rows - 1]

        own_sweeps(lambda row: field[step, row], wide, rows, store)

    @pl.loop(0, steps)
    def _(lag):
        for row in range(rows):
            turned[lag, row] = kern[lag, row].T
        for spot, row in enumerate(listed):
            outward[lag, :, spot * cols : (spot + 1) * cols] = kern[lag, row]

    for step in range(0, steps, 2):
        acc = None
        for lag in range(step + 2):
            left = jnp.concatenate([kern[lag, row] for row in range(HALO, rows - HALO)], axis=1)
            term = jnp.dot(left, pairs[step + 1 - lag], preferred_element_type=jnp.float32)
            acc = term if acc is None else acc + term
        data[step] = acc[:, 0:width]
        data[step + 1] = acc[:, width : 2 * width]


def before(field, diag, couple, kern, after):
    steps, rows, cols, width = field.shape
    sensors = kern.shape[2]
    inner = (rows - 2 * HALO) * cols
    return call(
        before_kernel,
        "before",
        (
            f32(steps, 2 * HALO, cols, width),
            f32(steps, 2, cols, width),
            f32(steps, sensors, width),
            bf16(steps, rows, cols, sensors),
            bf16(steps, sensors, 2 * HALO * cols),
        ),
        [VMEM] * 4 + [HBM],
        [VMEM] * 5,
        coef_scratch(rows + 2 * HALO, cols, width) + [pltpu.VMEM((steps + 1, inner, 2 * width), jnp.bfloat16)],
        12,
    )(field, diag, couple, kern, after)


def edge_product(half, pairs, outward, start, out):
    steps, sensors, _ = outward.shape
    width = out.shape[2]
    kept = sensors // 2
    span = pl.ds(pl.multiple_of(half * kept, kept), kept)
    for step in range(0, steps, 2):
        acc = jnp.concatenate([start[step, span, :], start[step + 1, span, :]], axis=1)
        for lag in range(step + 2):
            left = outward[lag, span, :]
            acc = acc + jnp.dot(left, pairs[step + 1 - lag], preferred_element_type=jnp.float32)
        out[step] = acc[:, 0:width].astype(out.dtype)
        out[step + 1] = acc[:, width : 2 * width].astype(out.dtype)


def leaving_kernel(
    twin, top, bottom, diag, couple, ctop, cbottom, edges, scaled, outward, start, out, pairs, line, wide, mix
):
    steps = outward.shape[0]
    cols, width = edges.shape[2], edges.shape[3]
    spread((diag, couple), (ctop, cbottom), line, wide)
    mix_coefs(wide, mix)
    pairs[0, :, 0:width] = jnp.zeros((2 * HALO * cols, width), pairs.dtype)

    @pl.loop(0, steps)
    def _(step):
        for side, message in enumerate((top, bottom)):
            added = halo_part(message, step * (HALO * cols), scaled[step, side], mix, side)
            for spot, extra in zip(spots_of(side), added):
                rounded = (edges[step, spot] + extra).astype(pairs.dtype)
                at = spot * cols
                pairs[step, at : at + cols, width : 2 * width] = rounded
                pairs[step + 1, at : at + cols, 0:width] = rounded

    edge_product(1 - twin[0], pairs, outward, start, out)


def leaving(twin, top, bottom, diag, couple, ctop, cbottom, edges, scaled, outward, start):
    steps, sensors, _ = outward.shape
    rows, cols = diag.shape
    width = edges.shape[3]
    return call(
        leaving_kernel,
        "leaving",
        [bf16(steps, sensors // 2, width), bf16(steps + 1, 2 * HALO * cols, 2 * width)],
        [SMEM] + [VMEM] * 10,
        [VMEM] * 2,
        coef_scratch(rows + 2 * HALO, cols, width) + [pltpu.VMEM((2, 8, cols, width), jnp.float32)],
        1,
    )(twin, top, bottom, diag, couple, ctop, cbottom, edges, scaled, outward, start)


def staying_kernel(twin, pairs, outward, start, out):
    edge_product(twin[0], pairs, outward, start, out)


def staying(twin, pairs, outward, start):
    steps, sensors, width = start.shape
    out = f32(steps, sensors // 2, width)
    return call(staying_kernel, "staying", out, [SMEM] + [VMEM] * 3, VMEM, [], 1)(twin, pairs, outward, start)


def join_kernel(mine, got, both):
    both[...] = (mine[...] + got[...].astype(jnp.float32)).astype(both.dtype)


def join(mine, got):
    return call(join_kernel, "join", bf16(*got.shape), [VMEM] * 2, VMEM, [], 1)(mine, got)


def scale_kernel(pieces, prec, out):
    total = pieces[0].astype(jnp.float32)
    for piece in range(1, pieces.shape[0]):
        total = total + pieces[piece].astype(jnp.float32)
    weighted = (total * prec[...]).astype(out.dtype)
    for piece in range(pieces.shape[0]):
        out[piece] = weighted


def scale(pieces, prec):
    return call(scale_kernel, "scale", bf16(*pieces.shape), [VMEM] * 2, VMEM, [], 1)(pieces, prec)


def fill_half(source, pairs):
    groups, share, width = source.shape
    kept = pairs.shape[1]
    steps = groups * share // kept
    pairs[steps, :, width : 2 * width] = jnp.zeros((kept, width), pairs.dtype)
    for piece in range(groups):
        step, first = divmod(piece * share, kept)
        value = source[groups - 1 - piece]
        pairs[step + 1, first : first + share, 0:width] = value
        pairs[step, first : first + share, width : 2 * width] = value


def half_product(rows, turned, half, pairs, step, acc):
    steps, _, cols, sensors = turned.shape
    kept = sensors // 2
    span = pl.ds(pl.multiple_of(half * kept, kept), kept)
    for lag in range(steps - step):
        left = turned[lag, rows, :, span].reshape((rows.stop - rows.start) * cols, kept)
        term = jnp.dot(left, pairs[step + lag + 1], preferred_element_type=jnp.float32)
        acc = term if acc is None else acc + term
    return acc


def strip_product(rows, turned, half, pairs, begun, field, message):
    steps, _, cols, _ = turned.shape
    strip = HALO * cols
    width = message.shape[1]
    for step in range(0, steps, 2):
        acc = half_product(rows, turned, half, pairs, step, begun[step // 2])
        for side in range(2):
            part = acc[:, side * width : (side + 1) * width]
            field[step + side] = part.reshape(HALO, cols, width)
            at = (step + side) * strip
            message[at : at + strip, :] = part.astype(message.dtype)


def own_kernel(twin, mine, turned, tail, head, pairs):
    steps, rows = turned.shape[0], turned.shape[1]
    fill_half(mine, pairs)
    for strip, out in ((slice(rows - HALO, rows), tail), (slice(0, HALO), head)):
        for step in range(0, steps, 2):
            out[step // 2] = half_product(strip, turned, twin[0], pairs, step, None)


def adjoint_own(twin, mine, turned):
    steps, _, cols, sensors = turned.shape
    width = mine.shape[2]
    strip = f32(steps // 2, HALO * cols, 2 * width)
    return call(
        own_kernel,
        "adjoint_own",
        (strip, strip, bf16(steps + 1, sensors // 2, 2 * width)),
        [SMEM] + [VMEM] * 2,
        [VMEM] * 3,
        [],
        4,
    )(twin, mine, turned)


def tail_kernel(twin, other, turned, begun, field, message, pairs):
    rows = turned.shape[1]
    fill_half(other, pairs)
    strip_product(slice(rows - HALO, rows), turned, 1 - twin[0], pairs, begun, field, message)


def head_kernel(twin, pairs, turned, begun, _, field, message):
    strip_product(slice(0, HALO), turned, 1 - twin[0], pairs, begun, field, message)


def adjoint_tail(twin, other, turned, begun):
    steps, _, cols, sensors = turned.shape
    width = other.shape[2]
    return call(
        tail_kernel,
        "adjoint_tail",
        (
            f32(steps, HALO, cols, width),
            bf16(steps * HALO * cols, width),
            bf16(steps + 1, sensors // 2, 2 * width),
        ),
        [SMEM] + [VMEM] * 3,
        [VMEM] * 3,
        [],
        4,
    )(twin, other, turned, begun)


def adjoint_head(twin, pairs, turned, begun, after):
    steps, _, cols, _ = turned.shape
    width = pairs.shape[2] // 2
    return call(
        head_kernel,
        "adjoint_head",
        (f32(steps, HALO, cols, width), bf16(steps * HALO * cols, width)),
        [SMEM, VMEM, VMEM, VMEM, HBM],
        [VMEM] * 2,
        [],
        4,
    )(twin, pairs, turned, begun, after)


def inner_kernel(
    twin, own, got, turned, upper, lower, diag, couple, ctop, cbottom, edges, scaled, out, mix, core, line, wide
):
    steps, rows, cols, sensors = turned.shape
    width = core.shape[3]
    inner = rows - 2 * HALO
    pack_at = pl.program_id(0)

    @pl.when(pack_at == 0)
    def _():
        spread((diag, couple), (ctop, cbottom), line, wide)
        mix_coefs(wide, mix)
        for step in range(0, steps, 2):
            acc = None
            for pairs, half in ((own, twin[0]), (got, 1 - twin[0])):
                acc = half_product(slice(HALO, rows - HALO), turned, half, pairs, step, acc)
            for side in range(2):
                core[step + side] = acc[:, side * width : (side + 1) * width].reshape(inner, cols, width)

    listed = edge_rows(rows)
    span = out.shape[0]

    @pl.loop(0, span)
    def _(at):
        step = pack_at * span + at

        def load(row):
            if row < HALO:
                return upper[step, row]
            return core[step, row - HALO] if row < rows - HALO else lower[step, row - rows + HALO]

        def store(row, value, weighted):
            if row in listed:
                edges[step, listed.index(row)] = value
            else:
                out[at, row - HALO] = value
            if row == 0:
                scaled[step, 0] = weighted[0]
            if row == rows - 1:
                scaled[step, 1] = weighted[rows - 1]

        own_sweeps(load, wide, rows, store)


def inner(twin, own, got, turned, upper, lower, diag, couple, ctop, cbottom):
    steps, rows, cols, _ = turned.shape
    width = upper.shape[3]
    core = rows - 2 * HALO
    assert core == HALO
    span = steps // 2
    return call(
        inner_kernel,
        "inner",
        (
            f32(steps, 2 * HALO, cols, width),
            f32(steps, 2, cols, width),
            f32(steps, rows, cols, width),
            f32(2, 8, cols, width),
        ),
        [SMEM] + [VMEM] * 9,
        [VMEM, VMEM, pl.BlockSpec((span, core, cols, width), lambda step: (step, 1, 0, 0)), VMEM],
        [pltpu.VMEM((steps, core, cols, width), jnp.float32)] + coef_scratch(rows + 2 * HALO, cols, width),
        10,
        (steps // span,),
    )(twin, own, got, turned, upper, lower, diag, couple, ctop, cbottom)


def finish_kernel(side, message, mix, edges, scaled, _, out):
    span, _, cols, _ = out.shape
    first = pl.program_id(0) * span

    @pl.loop(0, span)
    def _(at):
        step = first + at
        added = halo_part(message, step * (HALO * cols), scaled[step, side], mix, side)
        for spot, extra in zip(spots_of(side), added):
            out[at, spot % HALO] = edges[step, spot] + extra


def finish(side, message, mix, edges, scaled, out):
    steps, rows, cols, width = out.shape
    span = steps // 2
    place = side * (rows // HALO - 1)
    return call(
        functools.partial(finish_kernel, side),
        "finish",
        f32(*out.shape),
        [VMEM] * 4 + [HBM],
        pl.BlockSpec((span, HALO, cols, width), lambda step: (step, place, 0, 0)),
        [],
        2,
        (steps // span,),
        {4: 0},
    )(message, mix, edges, scaled, out)


def send_down(tail):
    return lax.ppermute(tail, "tile", [(i, i + 1) for i in range(lax.axis_size("tile") - 1)])


def send_up(head):
    return lax.ppermute(head, "tile", [(i + 1, i) for i in range(lax.axis_size("tile") - 1)])


def swap_twins(value):
    return lax.ppermute(value, "twin", [(0, 1), (1, 0)])


def body(sketch, diag_coef, couple, kernel, noise_prec):
    steps, _, rows, cols, width = sketch.shape
    sensors = kernel.shape[1]
    others = ("pair", "tile")
    groups = lax.axis_size(others)
    twin = lax.axis_index("twin")
    which = twin.reshape(1)
    field = sketch.reshape(steps, rows, cols, width)
    diag, couple = diag_coef.reshape(rows, cols), couple.reshape(rows, cols)
    kern = jnp.transpose(kernel.reshape(steps, sensors, rows, cols), (0, 2, 1, 3))
    kept = sensors // 2
    share = steps * kept // groups

    tail = pack(rows - HALO, field, sketch)
    top = send_down(tail)
    bottom = send_up(pack(0, field, tail))
    coefs = jnp.stack([diag, couple])
    note = send_down(coefs[:, rows - HALO :]), send_up(coefs[:, :HALO])
    noise = lax.dynamic_slice(noise_prec, (0, twin * kept), (steps, kept)).reshape(steps * kept)
    noise = lax.dynamic_slice(noise, (lax.axis_index(others) * share,), (share,))
    prec = jnp.broadcast_to(noise[:, None], (share, width))
    edges, scaled, data, turned, outward = before(field, diag, couple, kern, prec)

    gone, pairs = leaving(which, top, bottom, diag, couple, *note, edges, scaled, outward, data)
    both = join(staying(which, pairs, outward, data), swap_twins(gone)).reshape(groups, share, width)
    pieces = lax.all_to_all(both, others, 0, 0, tiled=True)
    backwards = [list(reversed(range(groups)))]
    weighted = lax.all_to_all(scale(pieces, prec), others, 0, 0, axis_index_groups=backwards, tiled=True)
    other = swap_twins(weighted)
    tail, head, own = adjoint_own(which, weighted, turned)
    lower, tail, got = adjoint_tail(which, other, turned, tail)
    top = send_down(tail)
    upper, head = adjoint_head(which, got, turned, head, tail)
    bottom = send_up(head)
    edges, scaled, out, mix = inner(which, own, got, turned, upper, lower, diag, couple, *note)
    out = finish(0, top, mix, edges, scaled, out)
    out = finish(1, bottom, mix, edges, scaled, out)
    return out.reshape(sketch.shape)


def solution(mesh):
    bands, tiles = mesh.shape["band"], mesh.shape["tile"]
    fine = Mesh(mesh.devices.reshape(bands // 2, 2, tiles), ("pair", "twin", "tile"))
    band = ("pair", "twin")
    placed = (
        P(None, band, "tile", None, None),
        P(band, "tile", None),
        P(band, "tile", None),
        P(None, None, band, "tile", None),
        P(),
    )
    return jax.shard_map(
        body,
        mesh=fine,
        in_specs=placed,
        out_specs=P(None, band, "tile", None, None),
        check_vma=False,
    )
```

profile of v0, /device:TPU:0, one launch (start us, length us, event | category | flops | bytes accessed | tf_op | source)
XLA Modules:
  0.0 106.8 jit_solution(12651852621876854966)
XLA Ops:
  0.0 2.1 %pack.2._ = bf16[2048,128]{1,0:T(8,128)(2,1)} custom-call(f32[8,6,128,128]{3,2,1,0:T(8,128)} %bitcast.16, f32[8,1,6,128,128]{4,3,2,1,0:T(8,128)} %_.1), custom_call_target="tpu_custom_call" | custom-call | bytes 3145728 | tf_op jit(solution)/shard_map/pack/pallas_call | solution.py:148
  2.1 0.0 copy-start.3
  2.1 0.0 copy-start.4
  2.1 4.9 %collective-permute-start = (bf16[2048,128]{1,0:T(8,128)(2,1)}, bf16[2048,128]{1,0:T(8,128)(2,1)S(1)}, u32[]{:S(2)}, u32[]{:S(2)}) collective-permute-start(bf16[2048,128]{1,0:T(8,128)(2,1)} %pack.2._), channel_id=1, source_target_pairs={{0,1},{1,2},{2,3},{3,4},{4,5},{5,6},{6,7},{8,9},{9,10},{10,11},{11... | collective-permute-start | bytes 1572872 | tf_op jit(solution)/shard_map/ppermute | solution.py:507
  7.0 2.0 %pack.3 = bf16[2048,128]{1,0:T(8,128)(2,1)} custom-call(f32[8,6,128,128]{3,2,1,0:T(8,128)} %bitcast.17, bf16[2048,128]{1,0:T(8,128)(2,1)} %pack.2._), custom_call_target="tpu_custom_call" | custom-call | bytes 3145728 | tf_op jit(solution)/shard_map/pack/pallas_call | solution.py:148
  9.0 1.3 %collective-permute-start.1 = (bf16[2048,128]{1,0:T(8,128)(2,1)}, bf16[2048,128]{1,0:T(8,128)(2,1)S(1)}, u32[]{:S(2)}, u32[]{:S(2)}) collective-permute-start(bf16[2048,128]{1,0:T(8,128)(2,1)} %pack.3), channel_id=1, source_target_pairs={{1,0},{2,1},{3,2},{4,3},{5,4},{6,5},{7,6},{9,8},{10,9},{11,10},{12... | collective-permute-start | bytes 1572872 | tf_op jit(solution)/shard_map/ppermute | solution.py:511
  10.4 1.3 %collective-permute-start.3 = (f32[2,2,128]{2,1,0:T(2,128)S(1)}, f32[2,2,128]{2,1,0:T(2,128)S(1)}, u32[]{:S(2)}, u32[]{:S(2)}) collective-permute-start(f32[2,2,128]{2,1,0:T(2,128)S(1)} %get-tuple-element.43), channel_id=1, source_target_pairs={{1,0},{2,1},{3,2},{4,3},{5,4},{6,5},{7,6},{9,8},{10,9},{11,10},{12... | collective-permute-start | bytes 6152 | tf_op jit(solution)/shard_map/ppermute | solution.py:511
  11.7 5.2 %collective-permute-start.2 = (f32[2,2,128]{2,1,0:T(2,128)S(1)}, f32[2,2,128]{2,1,0:T(2,128)S(1)}, u32[]{:S(2)}, u32[]{:S(2)}) collective-permute-start(f32[2,2,128]{2,1,0:T(2,128)S(1)} %get-tuple-element.44), channel_id=1, source_target_pairs={{0,1},{1,2},{2,3},{3,4},{4,5},{5,6},{6,7},{8,9},{9,10},{10,11},{11... | collective-permute-start | bytes 6152 | tf_op jit(solution)/shard_map/ppermute | solution.py:507
  16.9 0.1 dynamic_slice.7
  17.0 0.1 broadcast_in_dim.2._.prec
  17.1 1.9 %copy-done.1 = f32[8,1,6,128,128]{4,3,2,1,0:T(8,128)S(1)} copy-done((f32[8,1,6,128,128]{4,3,2,1,0:T(8,128)S(1)}, f32[8,1,6,128,128]{4,3,2,1,0:T(8,128)}, u32[]{:S(2)}) %copy-start.1) | copy-done | bytes 3145752
  19.0 2.8 %copy-done.2 = bf16[8,512,1,6,128]{4,1,3,2,0:T(8,128)(2,1)S(1)} copy-done((bf16[8,512,1,6,128]{4,1,3,2,0:T(8,128)(2,1)S(1)}, bf16[8,512,1,6,128]{4,1,3,2,0:T(8,128)(2,1)}, u32[]{:S(2)}) %copy-start.2) | copy-done | bytes 6291480
  21.8 7.2 %before.1 = (f32[8,4,128,128]{3,2,1,0:T(8,128)S(1)}, f32[8,2,128,128]{3,2,1,0:T(8,128)S(1)}, f32[8,512,128]{2,1,0:T(8,128)S(1)}, bf16[8,6,128,512]{3,2,1,0:T(8,128)(2,1)S(1)}, bf16[8,512,512]{2,1,0:T(8,128)(2,1)S(1)}) custom-call(f32[8,6,128,128]{3,2,1,0:T(8,128)S(1)} %bitcast.18, f32[6,128]{1,0:T(8,128)S(1)} %get-tuple-element.48.diag, ...), custom_call_target="tpu_custom_call" | custom-call | bytes 12582912 | tf_op jit(solution)/shard_map/before/pallas_call | solution.py:210
  28.9 0.8 collective-permute-done.2.ctop
  29.7 3.0 %leaving.1 = (bf16[8,256,128]{2,1,0:T(8,128)(2,1)S(1)}, bf16[9,512,256]{2,1,0:T(8,128)(2,1)S(1)}) custom-call(s32[1]{0:T(128)} %bitcast.twin, bf16[2048,128]{1,0:T(8,128)(2,1)S(1)} %collective-permute-done.top, bf16[2048,128]{1,0:T(8,128)(2,1)S(1)} %collective-permute-done.1.bottom, f32[6,128]{1,0:T(8,128)S(1)} %get-tuple-element.48.diag, ...), custom_call_target="tpu_custom_call" | custom-call | bytes 1048576 | tf_op jit(solution)/shard_map/leaving/pallas_call | solution.py:267
  32.8 0.1 collective-permute-start.4
  32.9 1.5 %staying.1.mine = f32[8,256,128]{2,1,0:T(8,128)S(1)} custom-call(s32[1]{0:T(128)} %bitcast.twin, bf16[9,512,256]{2,1,0:T(8,128)(2,1)S(1)} %get-tuple-element.28.pairs, bf16[8,512,512]{2,1,0:T(8,128)(2,1)S(1)} %get-tuple-element.26.outward, f32[8,512,128]{2,1,0:T(8,128)S(1)} %get-tuple-element.27.start), custom_call_target="tpu_custom_call" | custom-call | bytes 1048576 | tf_op jit(solution)/shard_map/staying/pallas_call | solution.py:285
  34.4 0.4 collective-permute-done.4.got
  34.7 0.1 join.1
  34.8 22.9 %all_to_all.10.pieces = bf16[16,128,128]{2,1,0:T(8,128)(2,1)S(1)} all-to-all(bf16[16,128,128]{2,1,0:T(8,128)(2,1)S(1)} %bitcast.20), channel_id=1, replica_groups=mesh['pair'=2,'twin'=2,'tile'=8] {'pair','tile'}, dimensions={0} | all-to-all | bytes 1048576 | tf_op jit(solution)/shard_map/all_to_all | solution.py:543
  57.8 0.1 scale.1
  57.9 17.0 %all_to_all.11.mine = bf16[16,128,128]{2,1,0:T(8,128)(2,1)S(1)} all-to-all(bf16[16,128,128]{2,1,0:T(8,128)(2,1)S(1)} %scale.1), channel_id=1, replica_groups={{23,22,21,20,19,18,17,16,7,6,5,4,3,2,1,0},{31,30,29,28,27,26,25,24,15,1..., dimensions={0} | all-to-all | bytes 1048576 | tf_op jit(solution)/shard_map/all_to_all | solution.py:545
  74.9 1.6 %adjoint_own.1 = (f32[4,256,256]{2,1,0:T(8,128)S(1)}, f32[4,256,256]{2,1,0:T(8,128)S(1)}, bf16[9,256,256]{2,1,0:T(8,128)(2,1)S(1)}) custom-call(s32[1]{0:T(128)} %bitcast.twin, bf16[16,128,128]{2,1,0:T(8,128)(2,1)S(1)} %all_to_all.11.mine, bf16[8,6,128,512]{3,2,1,0:T(8,128)(2,1)S(1)} %get-tuple-element.30.turned), custom_call_target="tpu_custom_call" | custom-call | bytes 4194304 | tf_op jit(solution)/shard_map/adjoint_own/pallas_call | solution.py:357
  76.5 0.3 collective-permute-done.5.other
  76.8 0.9 adjoint_tail.1
  77.7 3.7 %collective-permute-start.7 = (bf16[2048,128]{1,0:T(8,128)(2,1)S(1)}, bf16[2048,128]{1,0:T(8,128)(2,1)S(1)}, u32[]{:S(2)}, u32[]{:S(2)}) collective-permute-start(bf16[2048,128]{1,0:T(8,128)(2,1)S(1)} %get-tuple-element.34._), channel_id=1, source_target_pairs={{0,1},{1,2},{2,3},{3,4},{4,5},{5,6},{6,7},{8,9},{9,10},{10,11},{11... | collective-permute-start | bytes 1572872 | tf_op jit(solution)/shard_map/ppermute | solution.py:507
  81.4 0.9 adjoint_head.1
  82.2 1.3 %collective-permute-start.6 = (bf16[2048,128]{1,0:T(8,128)(2,1)S(1)}, bf16[2048,128]{1,0:T(8,128)(2,1)S(1)}, u32[]{:S(2)}, u32[]{:S(2)}) collective-permute-start(bf16[2048,128]{1,0:T(8,128)(2,1)S(1)} %get-tuple-element.35), channel_id=1, source_target_pairs={{1,0},{2,1},{3,2},{4,3},{5,4},{6,5},{7,6},{9,8},{10,9},{11,10},{12... | collective-permute-start | bytes 1572872 | tf_op jit(solution)/shard_map/ppermute | solution.py:511
  83.5 4.7 %inner.1 = (f32[8,4,128,128]{3,2,1,0:T(8,128)S(1)}, f32[8,2,128,128]{3,2,1,0:T(8,128)S(1)}, f32[8,6,128,128]{3,2,1,0:T(8,128)}, f32[2,8,128,128]{3,2,1,0:T(8,128)S(1)}) custom-call(s32[1]{0:T(128)} %bitcast.twin, bf16[9,256,256]{2,1,0:T(8,128)(2,1)S(1)} %get-tuple-element.36.own, bf16[9,256,256]{2,1,0:T(8,128)(2,1)S(1)} %get-tuple-element.32.pairs.got, ...), custom_call_target="tpu_custom_call" | custom-call | bytes 10485760 | tf_op jit(solution)/shard_map/inner/pallas_call | solution.py:460
  88.2 15.9 %collective-permute-done.7.message = bf16[2048,128]{1,0:T(8,128)(2,1)S(1)} collective-permute-done((bf16[2048,128]{1,0:T(8,128)(2,1)S(1)}, bf16[2048,128]{1,0:T(8,128)(2,1)S(1)}, u32[]{:S(2)}, u32[]{:S(2)}) %collective-permute-start.7) | collective-permute-done | bytes 524320 | tf_op jit(solution)/shard_map/ppermute | solution.py:507
  104.1 1.3 %finish.2._ = f32[8,6,128,128]{3,2,1,0:T(8,128)} custom-call(bf16[2048,128]{1,0:T(8,128)(2,1)S(1)} %collective-permute-done.7.message, f32[2,8,128,128]{3,2,1,0:T(8,128)S(1)} %get-tuple-element.39.mix, f32[8,4,128,128]{3,2,1,0:T(8,128)S(1)} %get-tuple-element.40.edges, ...), custom_call_target="tpu_custom_call", output_to_operand_aliasing={{}: (4, {})} | custom-call | bytes 2097152 | tf_op jit(solution)/shard_map/finish/pallas_call | solution.py:493
  105.4 1.3 %finish.3 = f32[8,6,128,128]{3,2,1,0:T(8,128)} custom-call(bf16[2048,128]{1,0:T(8,128)(2,1)S(1)} %collective-permute-done.6.message, f32[2,8,128,128]{3,2,1,0:T(8,128)S(1)} %get-tuple-element.39.mix, f32[8,4,128,128]{3,2,1,0:T(8,128)S(1)} %get-tuple-element.40.edges, ...), custom_call_target="tpu_custom_call", output_to_operand_aliasing={{}: (4, {})} | custom-call | bytes 2097152 | tf_op jit(solution)/shard_map/finish/pallas_call | solution.py:493
  (16 shorter events, 0.0 us)
Async XLA Ops:
  0.0 16.9 %copy-start = (f32[8,512]{1,0:T(8,128)S(1)}, f32[8,512]{1,0:T(8,128)}, u32[]{:S(2)}) copy-start(f32[8,512]{1,0:T(8,128)} %param.9) | copy-start | bytes 49156
  2.1 8.3 %copy-start.3 = (f32[1,6,128]{2,0,1:T(1,128)S(1)}, f32[1,6,128]{2,0,1:T(1,128)}, u32[]{:S(2)}) copy-start(f32[1,6,128]{2,0,1:T(1,128)} %param.6) | copy-start | bytes 9220
  2.1 8.3 %copy-start.4 = (f32[1,6,128]{2,0,1:T(1,128)S(1)}, f32[1,6,128]{2,0,1:T(1,128)}, u32[]{:S(2)}) copy-start(f32[1,6,128]{2,0,1:T(1,128)} %param.7) | copy-start | bytes 9220
  2.1 27.6 %collective-permute-start = (bf16[2048,128]{1,0:T(8,128)(2,1)}, bf16[2048,128]{1,0:T(8,128)(2,1)S(1)}, u32[]{:S(2)}, u32[]{:S(2)}) collective-permute-start(bf16[2048,128]{1,0:T(8,128)(2,1)} %pack.2._), channel_id=1, source_target_pairs={{0,1},{1,2},{2,3},{3,4},{4,5},{5,6},{6,7},{8,9},{9,10},{10,11},{11... | collective-permute-start | bytes 1572872 | tf_op jit(solution)/shard_map/ppermute | solution.py:507
  9.0 20.7 %collective-permute-start.1 = (bf16[2048,128]{1,0:T(8,128)(2,1)}, bf16[2048,128]{1,0:T(8,128)(2,1)S(1)}, u32[]{:S(2)}, u32[]{:S(2)}) collective-permute-start(bf16[2048,128]{1,0:T(8,128)(2,1)} %pack.3), channel_id=1, source_target_pairs={{1,0},{2,1},{3,2},{4,3},{5,4},{6,5},{7,6},{9,8},{10,9},{11,10},{12... | collective-permute-start | bytes 1572872 | tf_op jit(solution)/shard_map/ppermute | solution.py:511
  10.4 18.5 %collective-permute-start.3 = (f32[2,2,128]{2,1,0:T(2,128)S(1)}, f32[2,2,128]{2,1,0:T(2,128)S(1)}, u32[]{:S(2)}, u32[]{:S(2)}) collective-permute-start(f32[2,2,128]{2,1,0:T(2,128)S(1)} %get-tuple-element.43), channel_id=1, source_target_pairs={{1,0},{2,1},{3,2},{4,3},{5,4},{6,5},{7,6},{9,8},{10,9},{11,10},{12... | collective-permute-start | bytes 6152 | tf_op jit(solution)/shard_map/ppermute | solution.py:511
  11.7 18.0 %collective-permute-start.2 = (f32[2,2,128]{2,1,0:T(2,128)S(1)}, f32[2,2,128]{2,1,0:T(2,128)S(1)}, u32[]{:S(2)}, u32[]{:S(2)}) collective-permute-start(f32[2,2,128]{2,1,0:T(2,128)S(1)} %get-tuple-element.44), channel_id=1, source_target_pairs={{0,1},{1,2},{2,3},{3,4},{4,5},{5,6},{6,7},{8,9},{9,10},{10,11},{11... | collective-permute-start | bytes 6152 | tf_op jit(solution)/shard_map/ppermute | solution.py:507
  17.1 1.9 %copy-start.1 = (f32[8,1,6,128,128]{4,3,2,1,0:T(8,128)S(1)}, f32[8,1,6,128,128]{4,3,2,1,0:T(8,128)}, u32[]{:S(2)}) copy-start(f32[8,1,6,128,128]{4,3,2,1,0:T(8,128)} %_.1) | copy-start | bytes 9437188
  19.0 2.8 %copy-start.2 = (bf16[8,512,1,6,128]{4,1,3,2,0:T(8,128)(2,1)S(1)}, bf16[8,512,1,6,128]{4,1,3,2,0:T(8,128)(2,1)}, u32[]{:S(2)}) copy-start(bf16[8,512,1,6,128]{4,1,3,2,0:T(8,128)(2,1)} %param.8) | copy-start | bytes 18874372
  32.8 2.0 %collective-permute-start.4 = (bf16[8,256,128]{2,1,0:T(8,128)(2,1)S(1)}, bf16[8,256,128]{2,1,0:T(8,128)(2,1)S(1)}, u32[]{:S(2)}, u32[]{:S(2)}) collective-permute-start(bf16[8,256,128]{2,1,0:T(8,128)(2,1)S(1)} %get-tuple-element.29), channel_id=1, source_target_pairs={{0,8},{8,0},{1,9},{9,1},{2,10},{10,2},{3,11},{11,3},{4,12},{12,4},... | collective-permute-start | bytes 1572872 | tf_op jit(solution)/shard_map/ppermute | solution.py:515
  74.9 1.9 %collective-permute-start.5 = (bf16[16,128,128]{2,1,0:T(8,128)(2,1)S(1)}, bf16[16,128,128]{2,1,0:T(8,128)(2,1)S(1)}, u32[]{:S(2)}, u32[]{:S(2)}) collective-permute-start(bf16[16,128,128]{2,1,0:T(8,128)(2,1)S(1)} %all_to_all.11.mine), channel_id=1, source_target_pairs={{0,8},{8,0},{1,9},{9,1},{2,10},{10,2},{3,11},{11,3},{4,12},{12,4},... | collective-permute-start | bytes 1572872 | tf_op jit(solution)/shard_map/ppermute | solution.py:515
  77.7 26.4 %collective-permute-start.7 = (bf16[2048,128]{1,0:T(8,128)(2,1)S(1)}, bf16[2048,128]{1,0:T(8,128)(2,1)S(1)}, u32[]{:S(2)}, u32[]{:S(2)}) collective-permute-start(bf16[2048,128]{1,0:T(8,128)(2,1)S(1)} %get-tuple-element.34._), channel_id=1, source_target_pairs={{0,1},{1,2},{2,3},{3,4},{4,5},{5,6},{6,7},{8,9},{9,10},{10,11},{11... | collective-permute-start | bytes 1572872 | tf_op jit(solution)/shard_map/ppermute | solution.py:507
  82.2 23.2 %collective-permute-start.6 = (bf16[2048,128]{1,0:T(8,128)(2,1)S(1)}, bf16[2048,128]{1,0:T(8,128)(2,1)S(1)}, u32[]{:S(2)}, u32[]{:S(2)}) collective-permute-start(bf16[2048,128]{1,0:T(8,128)(2,1)S(1)} %get-tuple-element.35), channel_id=1, source_target_pairs={{1,0},{2,1},{3,2},{4,3},{5,4},{6,5},{7,6},{9,8},{10,9},{11,10},{12... | collective-permute-start | bytes 1572872 | tf_op jit(solution)/shard_map/ppermute | solution.py:511
where the time goes:
time: 107 us
  blocking collectives  39.9 us (37%)
  Pallas kernels  26.7 us (25%)
  starting transfers between devices  17.7 us (17%)
  waiting for transfers between devices  17.3 us (16%)
  local copies, waits for them, and re-layouts  4.88 us (5%)
    all_to_all x1, blocking collectives, body(): pieces = lax.all_to_all(both, others, 0, 0, tiled=True)  22.9 us
    all_to_all x1, blocking collectives, body(): lax.all_to_all(scale(pieces, prec), others, 0, 0, axis_index_groups=backw...  17 us
    ppermute x3, waiting for transfers between devices, send_down(): lax.ppermute(tail, 'tile', [(i, i + 1) for i in range(lax.axis_size('tile...  16.7 us
    ppermute x3, starting transfers between devices, send_down(): lax.ppermute(tail, 'tile', [(i, i + 1) for i in range(lax.axis_size('tile...  13.7 us
    pallas_call x1, Pallas kernels, before(): call(before_kernel, 'before', (f32(steps, 2 * HALO, cols, width), f32(ste...  7.16 us
    unnamed x13, local copies, waits for them, and re-layouts  4.71 us
    pallas_call x1, Pallas kernels, inner(): call(inner_kernel, 'inner', (f32(steps, 2 * HALO, cols, width), f32(steps...  4.69 us
    pallas_call x2, Pallas kernels, pack(): call(functools.partial(pack_kernel, first), 'pack', bf16(steps * strip, w...  4.11 us
  transfers between devices with their start and end apart: 8, of which 4 were waited for; matrix products, arithmetic and copies ran while one was open for 0% of the time, Pallas kernels for 18%

commit v1 on v0

--- a/solution.py
+++ b/solution.py
@@ -534,15 +534,15 @@
     coefs = jnp.stack([diag, couple])
     note = send_down(coefs[:, rows - HALO :]), send_up(coefs[:, :HALO])
     noise = lax.dynamic_slice(noise_prec, (0, twin * kept), (steps, kept)).reshape(steps * kept)
-    noise = lax.dynamic_slice(noise, (lax.axis_index(others) * share,), (share,))
+    noise = lax.dynamic_slice(noise, ((groups - 1 - lax.axis_index(others)) * share,), (share,))
     prec = jnp.broadcast_to(noise[:, None], (share, width))
     edges, scaled, data, turned, outward = before(field, diag, couple, kern, prec)
 
     gone, pairs = leaving(which, top, bottom, diag, couple, *note, edges, scaled, outward, data)
     both = join(staying(which, pairs, outward, data), swap_twins(gone)).reshape(groups, share, width)
-    pieces = lax.all_to_all(both, others, 0, 0, tiled=True)
     backwards = [list(reversed(range(groups)))]
-    weighted = lax.all_to_all(scale(pieces, prec), others, 0, 0, axis_index_groups=backwards, tiled=True)
+    pieces = lax.all_to_all(both, others, 0, 0, axis_index_groups=backwards, tiled=True)
+    weighted = lax.all_to_all(scale(pieces, prec), others, 0, 0, tiled=True)
     other = swap_twins(weighted)
     tail, head, own = adjoint_own(which, weighted, turned)
     lower, tail, got = adjoint_tail(which, other, turned, tail)

time: 107 us -> 106 us (level)
  starting transfers between devices: 17.7 us -> 16.5 us
    ppermute x3, starting transfers between devices: 13.7 us -> 12.5 us  [send_down(): lax.ppermute(tail, 'tile', [(i, i + 1) for i in range(lax.axis_size('tile...]
where the time goes in v1:
time: 106 us; the launch traced here: 105 us
  blocking collectives  39.5 us (37%)
  Pallas kernels  27 us (25%)
  waiting for transfers between devices  17.2 us (16%)
  starting transfers between devices  16.5 us (16%)
  local copies, waits for them, and re-layouts  4.88 us (5%)
    all_to_all x1, blocking collectives, body(): lax.all_to_all(both, others, 0, 0, axis_index_groups=backwards, tiled=True)  20.7 us
    all_to_all x1, blocking collectives, body(): weighted = lax.all_to_all(scale(pieces, prec), others, 0, 0, tiled=True)  18.8 us
    ppermute x3, waiting for transfers between devices, send_down(): lax.ppermute(tail, 'tile', [(i, i + 1) for i in range(lax.axis_size('tile...  16.6 us
    ppermute x3, starting transfers between devices, send_down(): lax.ppermute(tail, 'tile', [(i, i + 1) for i in range(lax.axis_size('tile...  12.5 us
    pallas_call x1, Pallas kernels, before(): call(before_kernel, 'before', (f32(steps, 2 * HALO, cols, width), f32(ste...  7.19 us
    pallas_call x1, Pallas kernels, inner(): call(inner_kernel, 'inner', (f32(steps, 2 * HALO, cols, width), f32(steps...  4.76 us
    unnamed x13, local copies, waits for them, and re-layouts  4.71 us
    pallas_call x2, Pallas kernels, pack(): call(functools.partial(pack_kernel, first), 'pack', bf16(steps * strip, w...  4.11 us
  transfers between devices with their start and end apart: 8, of which 4 were waited for; matrix products, arithmetic and copies ran while one was open for 0% of the time, Pallas kernels for 18%

profile of v1, /device:TPU:0, one launch (start us, length us, event | category | flops | bytes accessed | tf_op | source)
XLA Modules:
  0.0 105.4 jit_solution(12214861303588640238)
XLA Ops:
  0.0 2.1 %pack.2._ = bf16[2048,128]{1,0:T(8,128)(2,1)} custom-call(f32[8,6,128,128]{3,2,1,0:T(8,128)} %bitcast.16, f32[8,1,6,128,128]{4,3,2,1,0:T(8,128)} %_.1), custom_call_target="tpu_custom_call" | custom-call | bytes 3145728 | tf_op jit(solution)/shard_map/pack/pallas_call | solution.py:148
  2.1 0.0 copy-start.3
  2.1 0.0 copy-start.4
  2.1 4.9 %collective-permute-start = (bf16[2048,128]{1,0:T(8,128)(2,1)}, bf16[2048,128]{1,0:T(8,128)(2,1)S(1)}, u32[]{:S(2)}, u32[]{:S(2)}) collective-permute-start(bf16[2048,128]{1,0:T(8,128)(2,1)} %pack.2._), channel_id=1, source_target_pairs={{0,1},{1,2},{2,3},{3,4},{4,5},{5,6},{6,7},{8,9},{9,10},{10,11},{11... | collective-permute-start | bytes 1572872 | tf_op jit(solution)/shard_map/ppermute | solution.py:507
  7.0 2.0 %pack.3 = bf16[2048,128]{1,0:T(8,128)(2,1)} custom-call(f32[8,6,128,128]{3,2,1,0:T(8,128)} %bitcast.17, bf16[2048,128]{1,0:T(8,128)(2,1)} %pack.2._), custom_call_target="tpu_custom_call" | custom-call | bytes 3145728 | tf_op jit(solution)/shard_map/pack/pallas_call | solution.py:148
  9.0 1.3 %collective-permute-start.1 = (bf16[2048,128]{1,0:T(8,128)(2,1)}, bf16[2048,128]{1,0:T(8,128)(2,1)S(1)}, u32[]{:S(2)}, u32[]{:S(2)}) collective-permute-start(bf16[2048,128]{1,0:T(8,128)(2,1)} %pack.3), channel_id=1, source_target_pairs={{1,0},{2,1},{3,2},{4,3},{5,4},{6,5},{7,6},{9,8},{10,9},{11,10},{12... | collective-permute-start | bytes 1572872 | tf_op jit(solution)/shard_map/ppermute | solution.py:511
  10.4 1.3 %collective-permute-start.3 = (f32[2,2,128]{2,1,0:T(2,128)S(1)}, f32[2,2,128]{2,1,0:T(2,128)S(1)}, u32[]{:S(2)}, u32[]{:S(2)}) collective-permute-start(f32[2,2,128]{2,1,0:T(2,128)S(1)} %get-tuple-element.43), channel_id=1, source_target_pairs={{1,0},{2,1},{3,2},{4,3},{5,4},{6,5},{7,6},{9,8},{10,9},{11,10},{12... | collective-permute-start | bytes 6152 | tf_op jit(solution)/shard_map/ppermute | solution.py:511
  11.7 5.2 %collective-permute-start.2 = (f32[2,2,128]{2,1,0:T(2,128)S(1)}, f32[2,2,128]{2,1,0:T(2,128)S(1)}, u32[]{:S(2)}, u32[]{:S(2)}) collective-permute-start(f32[2,2,128]{2,1,0:T(2,128)S(1)} %get-tuple-element.44), channel_id=1, source_target_pairs={{0,1},{1,2},{2,3},{3,4},{4,5},{5,6},{6,7},{8,9},{9,10},{10,11},{11... | collective-permute-start | bytes 6152 | tf_op jit(solution)/shard_map/ppermute | solution.py:507
  16.9 0.1 dynamic_slice.7
  17.0 0.1 broadcast_in_dim.2._.prec
  17.1 1.9 %copy-done.1 = f32[8,1,6,128,128]{4,3,2,1,0:T(8,128)S(1)} copy-done((f32[8,1,6,128,128]{4,3,2,1,0:T(8,128)S(1)}, f32[8,1,6,128,128]{4,3,2,1,0:T(8,128)}, u32[]{:S(2)}) %copy-start.1) | copy-done | bytes 3145752
  19.0 2.8 %copy-done.2 = bf16[8,512,1,6,128]{4,1,3,2,0:T(8,128)(2,1)S(1)} copy-done((bf16[8,512,1,6,128]{4,1,3,2,0:T(8,128)(2,1)S(1)}, bf16[8,512,1,6,128]{4,1,3,2,0:T(8,128)(2,1)}, u32[]{:S(2)}) %copy-start.2) | copy-done | bytes 6291480
  21.8 7.2 %before.1 = (f32[8,4,128,128]{3,2,1,0:T(8,128)S(1)}, f32[8,2,128,128]{3,2,1,0:T(8,128)S(1)}, f32[8,512,128]{2,1,0:T(8,128)S(1)}, bf16[8,6,128,512]{3,2,1,0:T(8,128)(2,1)S(1)}, bf16[8,512,512]{2,1,0:T(8,128)(2,1)S(1)}) custom-call(f32[8,6,128,128]{3,2,1,0:T(8,128)S(1)} %bitcast.18, f32[6,128]{1,0:T(8,128)S(1)} %get-tuple-element.48.diag, ...), custom_call_target="tpu_custom_call" | custom-call | bytes 12582912 | tf_op jit(solution)/shard_map/before/pallas_call | solution.py:210
  29.0 0.8 collective-permute-done.2.ctop
  29.7 3.2 %leaving.1 = (bf16[8,256,128]{2,1,0:T(8,128)(2,1)S(1)}, bf16[9,512,256]{2,1,0:T(8,128)(2,1)S(1)}) custom-call(s32[1]{0:T(128)} %bitcast.twin, bf16[2048,128]{1,0:T(8,128)(2,1)S(1)} %collective-permute-done.top, bf16[2048,128]{1,0:T(8,128)(2,1)S(1)} %collective-permute-done.1.bottom, f32[6,128]{1,0:T(8,128)S(1)} %get-tuple-element.48.diag, ...), custom_call_target="tpu_custom_call" | custom-call | bytes 1048576 | tf_op jit(solution)/shard_map/leaving/pallas_call | solution.py:267
  32.9 0.1 collective-permute-start.4
  33.0 1.5 %staying.1.mine = f32[8,256,128]{2,1,0:T(8,128)S(1)} custom-call(s32[1]{0:T(128)} %bitcast.twin, bf16[9,512,256]{2,1,0:T(8,128)(2,1)S(1)} %get-tuple-element.28.pairs, bf16[8,512,512]{2,1,0:T(8,128)(2,1)S(1)} %get-tuple-element.26.outward, f32[8,512,128]{2,1,0:T(8,128)S(1)} %get-tuple-element.27.start), custom_call_target="tpu_custom_call" | custom-call | bytes 1048576 | tf_op jit(solution)/shard_map/staying/pallas_call | solution.py:285
  34.5 0.4 collective-permute-done.4.got
  34.9 0.1 join.1
  35.0 20.7 %all_to_all.10.pieces = bf16[16,128,128]{2,1,0:T(8,128)(2,1)S(1)} all-to-all(bf16[16,128,128]{2,1,0:T(8,128)(2,1)S(1)} %bitcast.20), channel_id=1, replica_groups={{23,22,21,20,19,18,17,16,7,6,5,4,3,2,1,0},{31,30,29,28,27,26,25,24,15,1..., dimensions={0} | all-to-all | bytes 1048576 | tf_op jit(solution)/shard_map/all_to_all | solution.py:544
  55.7 0.1 scale.1
  55.8 18.8 %all_to_all.11.mine = bf16[16,128,128]{2,1,0:T(8,128)(2,1)S(1)} all-to-all(bf16[16,128,128]{2,1,0:T(8,128)(2,1)S(1)} %scale.1), channel_id=1, replica_groups=mesh['pair'=2,'twin'=2,'tile'=8] {'pair','tile'}, dimensions={0} | all-to-all | bytes 1048576 | tf_op jit(solution)/shard_map/all_to_all | solution.py:545
  74.6 1.6 %adjoint_own.1 = (f32[4,256,256]{2,1,0:T(8,128)S(1)}, f32[4,256,256]{2,1,0:T(8,128)S(1)}, bf16[9,256,256]{2,1,0:T(8,128)(2,1)S(1)}) custom-call(s32[1]{0:T(128)} %bitcast.twin, bf16[16,128,128]{2,1,0:T(8,128)(2,1)S(1)} %all_to_all.11.mine, bf16[8,6,128,512]{3,2,1,0:T(8,128)(2,1)S(1)} %get-tuple-element.30.turned), custom_call_target="tpu_custom_call" | custom-call | bytes 4194304 | tf_op jit(solution)/shard_map/adjoint_own/pallas_call | solution.py:357
  76.2 0.3 collective-permute-done.5.other
  76.5 0.9 adjoint_tail.1
  77.4 2.5 %collective-permute-start.7 = (bf16[2048,128]{1,0:T(8,128)(2,1)S(1)}, bf16[2048,128]{1,0:T(8,128)(2,1)S(1)}, u32[]{:S(2)}, u32[]{:S(2)}) collective-permute-start(bf16[2048,128]{1,0:T(8,128)(2,1)S(1)} %get-tuple-element.34._), channel_id=1, source_target_pairs={{0,1},{1,2},{2,3},{3,4},{4,5},{5,6},{6,7},{8,9},{9,10},{10,11},{11... | collective-permute-start | bytes 1572872 | tf_op jit(solution)/shard_map/ppermute | solution.py:507
  79.9 0.9 adjoint_head.1
  80.8 1.3 %collective-permute-start.6 = (bf16[2048,128]{1,0:T(8,128)(2,1)S(1)}, bf16[2048,128]{1,0:T(8,128)(2,1)S(1)}, u32[]{:S(2)}, u32[]{:S(2)}) collective-permute-start(bf16[2048,128]{1,0:T(8,128)(2,1)S(1)} %get-tuple-element.35), channel_id=1, source_target_pairs={{1,0},{2,1},{3,2},{4,3},{5,4},{6,5},{7,6},{9,8},{10,9},{11,10},{12... | collective-permute-start | bytes 1572872 | tf_op jit(solution)/shard_map/ppermute | solution.py:511
  82.1 4.8 %inner.1 = (f32[8,4,128,128]{3,2,1,0:T(8,128)S(1)}, f32[8,2,128,128]{3,2,1,0:T(8,128)S(1)}, f32[8,6,128,128]{3,2,1,0:T(8,128)}, f32[2,8,128,128]{3,2,1,0:T(8,128)S(1)}) custom-call(s32[1]{0:T(128)} %bitcast.twin, bf16[9,256,256]{2,1,0:T(8,128)(2,1)S(1)} %get-tuple-element.36.own, bf16[9,256,256]{2,1,0:T(8,128)(2,1)S(1)} %get-tuple-element.32.pairs.got, ...), custom_call_target="tpu_custom_call" | custom-call | bytes 10485760 | tf_op jit(solution)/shard_map/inner/pallas_call | solution.py:460
  86.9 15.8 %collective-permute-done.7.message = bf16[2048,128]{1,0:T(8,128)(2,1)S(1)} collective-permute-done((bf16[2048,128]{1,0:T(8,128)(2,1)S(1)}, bf16[2048,128]{1,0:T(8,128)(2,1)S(1)}, u32[]{:S(2)}, u32[]{:S(2)}) %collective-permute-start.7) | collective-permute-done | bytes 524320 | tf_op jit(solution)/shard_map/ppermute | solution.py:507
  102.7 1.3 %finish.2._ = f32[8,6,128,128]{3,2,1,0:T(8,128)} custom-call(bf16[2048,128]{1,0:T(8,128)(2,1)S(1)} %collective-permute-done.7.message, f32[2,8,128,128]{3,2,1,0:T(8,128)S(1)} %get-tuple-element.39.mix, f32[8,4,128,128]{3,2,1,0:T(8,128)S(1)} %get-tuple-element.40.edges, ...), custom_call_target="tpu_custom_call", output_to_operand_aliasing={{}: (4, {})} | custom-call | bytes 2097152 | tf_op jit(solution)/shard_map/finish/pallas_call | solution.py:493
  104.0 1.3 %finish.3 = f32[8,6,128,128]{3,2,1,0:T(8,128)} custom-call(bf16[2048,128]{1,0:T(8,128)(2,1)S(1)} %collective-permute-done.6.message, f32[2,8,128,128]{3,2,1,0:T(8,128)S(1)} %get-tuple-element.39.mix, f32[8,4,128,128]{3,2,1,0:T(8,128)S(1)} %get-tuple-element.40.edges, ...), custom_call_target="tpu_custom_call", output_to_operand_aliasing={{}: (4, {})} | custom-call | bytes 2097152 | tf_op jit(solution)/shard_map/finish/pallas_call | solution.py:493
  (16 shorter events, 0.0 us)
Async XLA Ops:
  0.0 16.9 %copy-start = (f32[8,512]{1,0:T(8,128)S(1)}, f32[8,512]{1,0:T(8,128)}, u32[]{:S(2)}) copy-start(f32[8,512]{1,0:T(8,128)} %param.9) | copy-start | bytes 49156
  2.1 8.3 %copy-start.3 = (f32[1,6,128]{2,0,1:T(1,128)S(1)}, f32[1,6,128]{2,0,1:T(1,128)}, u32[]{:S(2)}) copy-start(f32[1,6,128]{2,0,1:T(1,128)} %param.6) | copy-start | bytes 9220
  2.1 8.3 %copy-start.4 = (f32[1,6,128]{2,0,1:T(1,128)S(1)}, f32[1,6,128]{2,0,1:T(1,128)}, u32[]{:S(2)}) copy-start(f32[1,6,128]{2,0,1:T(1,128)} %param.7) | copy-start | bytes 9220
  2.1 27.6 %collective-permute-start = (bf16[2048,128]{1,0:T(8,128)(2,1)}, bf16[2048,128]{1,0:T(8,128)(2,1)S(1)}, u32[]{:S(2)}, u32[]{:S(2)}) collective-permute-start(bf16[2048,128]{1,0:T(8,128)(2,1)} %pack.2._), channel_id=1, source_target_pairs={{0,1},{1,2},{2,3},{3,4},{4,5},{5,6},{6,7},{8,9},{9,10},{10,11},{11... | collective-permute-start | bytes 1572872 | tf_op jit(solution)/shard_map/ppermute | solution.py:507
  9.0 20.7 %collective-permute-start.1 = (bf16[2048,128]{1,0:T(8,128)(2,1)}, bf16[2048,128]{1,0:T(8,128)(2,1)S(1)}, u32[]{:S(2)}, u32[]{:S(2)}) collective-permute-start(bf16[2048,128]{1,0:T(8,128)(2,1)} %pack.3), channel_id=1, source_target_pairs={{1,0},{2,1},{3,2},{4,3},{5,4},{6,5},{7,6},{9,8},{10,9},{11,10},{12... | collective-permute-start | bytes 1572872 | tf_op jit(solution)/shard_map/ppermute | solution.py:511
  10.4 18.6 %collective-permute-start.3 = (f32[2,2,128]{2,1,0:T(2,128)S(1)}, f32[2,2,128]{2,1,0:T(2,128)S(1)}, u32[]{:S(2)}, u32[]{:S(2)}) collective-permute-start(f32[2,2,128]{2,1,0:T(2,128)S(1)} %get-tuple-element.43), channel_id=1, source_target_pairs={{1,0},{2,1},{3,2},{4,3},{5,4},{6,5},{7,6},{9,8},{10,9},{11,10},{12... | collective-permute-start | bytes 6152 | tf_op jit(solution)/shard_map/ppermute | solution.py:511
  11.7 18.0 %collective-permute-start.2 = (f32[2,2,128]{2,1,0:T(2,128)S(1)}, f32[2,2,128]{2,1,0:T(2,128)S(1)}, u32[]{:S(2)}, u32[]{:S(2)}) collective-permute-start(f32[2,2,128]{2,1,0:T(2,128)S(1)} %get-tuple-element.44), channel_id=1, source_target_pairs={{0,1},{1,2},{2,3},{3,4},{4,5},{5,6},{6,7},{8,9},{9,10},{10,11},{11... | collective-permute-start | bytes 6152 | tf_op jit(solution)/shard_map/ppermute | solution.py:507
  17.1 1.9 %copy-start.1 = (f32[8,1,6,128,128]{4,3,2,1,0:T(8,128)S(1)}, f32[8,1,6,128,128]{4,3,2,1,0:T(8,128)}, u32[]{:S(2)}) copy-start(f32[8,1,6,128,128]{4,3,2,1,0:T(8,128)} %_.1) | copy-start | bytes 9437188
  19.0 2.8 %copy-start.2 = (bf16[8,512,1,6,128]{4,1,3,2,0:T(8,128)(2,1)S(1)}, bf16[8,512,1,6,128]{4,1,3,2,0:T(8,128)(2,1)}, u32[]{:S(2)}) copy-start(bf16[8,512,1,6,128]{4,1,3,2,0:T(8,128)(2,1)} %param.8) | copy-start | bytes 18874372
  32.9 2.0 %collective-permute-start.4 = (bf16[8,256,128]{2,1,0:T(8,128)(2,1)S(1)}, bf16[8,256,128]{2,1,0:T(8,128)(2,1)S(1)}, u32[]{:S(2)}, u32[]{:S(2)}) collective-permute-start(bf16[8,256,128]{2,1,0:T(8,128)(2,1)S(1)} %get-tuple-element.29), channel_id=1, source_target_pairs={{0,8},{8,0},{1,9},{9,1},{2,10},{10,2},{3,11},{11,3},{4,12},{12,4},... | collective-permute-start | bytes 1572872 | tf_op jit(solution)/shard_map/ppermute | solution.py:515
  74.6 1.9 %collective-permute-start.5 = (bf16[16,128,128]{2,1,0:T(8,128)(2,1)S(1)}, bf16[16,128,128]{2,1,0:T(8,128)(2,1)S(1)}, u32[]{:S(2)}, u32[]{:S(2)}) collective-permute-start(bf16[16,128,128]{2,1,0:T(8,128)(2,1)S(1)} %all_to_all.11.mine), channel_id=1, source_target_pairs={{0,8},{8,0},{1,9},{9,1},{2,10},{10,2},{3,11},{11,3},{4,12},{12,4},... | collective-permute-start | bytes 1572872 | tf_op jit(solution)/shard_map/ppermute | solution.py:515
  77.4 25.3 %collective-permute-start.7 = (bf16[2048,128]{1,0:T(8,128)(2,1)S(1)}, bf16[2048,128]{1,0:T(8,128)(2,1)S(1)}, u32[]{:S(2)}, u32[]{:S(2)}) collective-permute-start(bf16[2048,128]{1,0:T(8,128)(2,1)S(1)} %get-tuple-element.34._), channel_id=1, source_target_pairs={{0,1},{1,2},{2,3},{3,4},{4,5},{5,6},{6,7},{8,9},{9,10},{10,11},{11... | collective-permute-start | bytes 1572872 | tf_op jit(solution)/shard_map/ppermute | solution.py:507
  80.8 23.2 %collective-permute-start.6 = (bf16[2048,128]{1,0:T(8,128)(2,1)S(1)}, bf16[2048,128]{1,0:T(8,128)(2,1)S(1)}, u32[]{:S(2)}, u32[]{:S(2)}) collective-permute-start(bf16[2048,128]{1,0:T(8,128)(2,1)S(1)} %get-tuple-element.35), channel_id=1, source_target_pairs={{1,0},{2,1},{3,2},{4,3},{5,4},{6,5},{7,6},{9,8},{10,9},{11,10},{12... | collective-permute-start | bytes 1572872 | tf_op jit(solution)/shard_map/ppermute | solution.py:511

commit v2 on v1

--- a/solution.py
+++ b/solution.py
@@ -365,22 +365,22 @@
     )(twin, mine, turned)
 
 
-def tail_kernel(twin, other, turned, begun, field, message, pairs):
+def first_kernel(twin, other, turned, begun, field, message, pairs):
+    fill_half(other, pairs)
+    strip_product(slice(0, HALO), turned, 1 - twin[0], pairs, begun, field, message)
+
+
+def second_kernel(twin, pairs, turned, begun, _, field, message):
     rows = turned.shape[1]
-    fill_half(other, pairs)
     strip_product(slice(rows - HALO, rows), turned, 1 - twin[0], pairs, begun, field, message)
 
 
-def head_kernel(twin, pairs, turned, begun, _, field, message):
-    strip_product(slice(0, HALO), turned, 1 - twin[0], pairs, begun, field, message)
-
-
-def adjoint_tail(twin, other, turned, begun):
+def adjoint_first(twin, other, turned, begun):
     steps, _, cols, sensors = turned.shape
     width = other.shape[2]
     return call(
-        tail_kernel,
-        "adjoint_tail",
+        first_kernel,
+        "adjoint_first",
         (
             f32(steps, HALO, cols, width),
             bf16(steps * HALO * cols, width),
@@ -393,12 +393,12 @@
     )(twin, other, turned, begun)
 
 
-def adjoint_head(twin, pairs, turned, begun, after):
+def adjoint_second(twin, pairs, turned, begun, after):
     steps, _, cols, _ = turned.shape
     width = pairs.shape[2] // 2
     return call(
-        head_kernel,
-        "adjoint_head",
+        second_kernel,
+        "adjoint_second",
         (f32(steps, HALO, cols, width), bf16(steps * HALO * cols, width)),
         [SMEM, VMEM, VMEM, VMEM, HBM],
         [VMEM] * 2,
@@ -545,13 +545,13 @@
     weighted = lax.all_to_all(scale(pieces, prec), others, 0, 0, tiled=True)
     other = swap_twins(weighted)
     tail, head, own = adjoint_own(which, weighted, turned)
-    lower, tail, got = adjoint_tail(which, other, turned, tail)
+    upper, head, got = adjoint_first(which, other, turned, head)
+    bottom = send_up(head)
+    lower, tail = adjoint_second(which, got, turned, tail, head)
     top = send_down(tail)
-    upper, head = adjoint_head(which, got, turned, head, tail)
-    bottom = send_up(head)
     edges, scaled, out, mix = inner(which, own, got, turned, upper, lower, diag, couple, *note)
+    out = finish(1, bottom, mix, edges, scaled, out)
     out = finish(0, top, mix, edges, scaled, out)
-    out = finish(1, bottom, mix, edges, scaled, out)
     return out.reshape(sketch.shape)
 
 

time: 106 us -> 106 us (level)
  waiting for transfers between devices: 17.2 us -> 14.7 us
  starting transfers between devices: 16.5 us -> 18.6 us
    ppermute x3, waiting for transfers between devices: 16.6 us -> 9.63 us  [send_down(): lax.ppermute(tail, 'tile', [(i, i + 1) for i in range(lax.axis_size('tile...]
    ppermute x3, waiting for transfers between devices: 0.01 us -> 4.42 us  [send_up(): lax.ppermute(head, 'tile', [(i + 1, i) for i in range(lax.axis_size('tile...]
    ppermute x3, starting transfers between devices: 12.5 us -> 14.6 us  [send_down(): lax.ppermute(tail, 'tile', [(i, i + 1) for i in range(lax.axis_size('tile...]
  transfers between devices with their start and end apart: 8 -> 8, of which waited for: 4 -> 5; matrix products, arithmetic and copies ran while one was open for 0% -> 0% of each run, Pallas kernels for 18% -> 18%
where the time goes in v2:
time: 106 us; the launch traced here: 105 us
  blocking collectives  39.5 us (37%)
  Pallas kernels  27 us (25%)
  starting transfers between devices  18.6 us (18%)
  waiting for transfers between devices  14.7 us (14%)
  local copies, waits for them, and re-layouts  4.88 us (5%)
    all_to_all x1, blocking collectives, body(): lax.all_to_all(both, others, 0, 0, axis_index_groups=backwards, tiled=True)  20.7 us
    all_to_all x1, blocking collectives, body(): weighted = lax.all_to_all(scale(pieces, prec), others, 0, 0, tiled=True)  18.8 us
    ppermute x3, starting transfers between devices, send_down(): lax.ppermute(tail, 'tile', [(i, i + 1) for i in range(lax.axis_size('tile...  14.6 us
    ppermute x3, waiting for transfers between devices, send_down(): lax.ppermute(tail, 'tile', [(i, i + 1) for i in range(lax.axis_size('tile...  9.63 us
    pallas_call x1, Pallas kernels, before(): call(before_kernel, 'before', (f32(steps, 2 * HALO, cols, width), f32(ste...  7.19 us
    pallas_call x1, Pallas kernels, inner(): call(inner_kernel, 'inner', (f32(steps, 2 * HALO, cols, width), f32(steps...  4.76 us
    unnamed x13, local copies, waits for them, and re-layouts  4.71 us
    ppermute x3, waiting for transfers between devices, send_up(): lax.ppermute(head, 'tile', [(i + 1, i) for i in range(lax.axis_size('tile...  4.42 us
  transfers between devices with their start and end apart: 8, of which 5 were waited for; matrix products, arithmetic and copies ran while one was open for 0% of the time, Pallas kernels for 18%

profile of v2, /device:TPU:0, one launch (start us, length us, event | category | flops | bytes accessed | tf_op | source)
XLA Modules:
  0.0 104.9 jit_solution(6545622837871013245)
XLA Ops:
  0.0 2.1 %pack.2._ = bf16[2048,128]{1,0:T(8,128)(2,1)} custom-call(f32[8,6,128,128]{3,2,1,0:T(8,128)} %bitcast.16, f32[8,1,6,128,128]{4,3,2,1,0:T(8,128)} %_.1), custom_call_target="tpu_custom_call" | custom-call | bytes 3145728 | tf_op jit(solution)/shard_map/pack/pallas_call | solution.py:148
  2.1 0.0 copy-start.3
  2.1 4.9 %collective-permute-start = (bf16[2048,128]{1,0:T(8,128)(2,1)}, bf16[2048,128]{1,0:T(8,128)(2,1)S(1)}, u32[]{:S(2)}, u32[]{:S(2)}) collective-permute-start(bf16[2048,128]{1,0:T(8,128)(2,1)} %pack.2._), channel_id=1, source_target_pairs={{0,1},{1,2},{2,3},{3,4},{4,5},{5,6},{6,7},{8,9},{9,10},{10,11},{11... | collective-permute-start | bytes 1572872 | tf_op jit(solution)/shard_map/ppermute | solution.py:507
  7.0 2.0 %pack.3 = bf16[2048,128]{1,0:T(8,128)(2,1)} custom-call(f32[8,6,128,128]{3,2,1,0:T(8,128)} %bitcast.17, bf16[2048,128]{1,0:T(8,128)(2,1)} %pack.2._), custom_call_target="tpu_custom_call" | custom-call | bytes 3145728 | tf_op jit(solution)/shard_map/pack/pallas_call | solution.py:148
  9.0 1.3 %collective-permute-start.1 = (bf16[2048,128]{1,0:T(8,128)(2,1)}, bf16[2048,128]{1,0:T(8,128)(2,1)S(1)}, u32[]{:S(2)}, u32[]{:S(2)}) collective-permute-start(bf16[2048,128]{1,0:T(8,128)(2,1)} %pack.3), channel_id=1, source_target_pairs={{1,0},{2,1},{3,2},{4,3},{5,4},{6,5},{7,6},{9,8},{10,9},{11,10},{12... | collective-permute-start | bytes 1572872 | tf_op jit(solution)/shard_map/ppermute | solution.py:511
  10.4 1.3 %collective-permute-start.3 = (f32[2,2,128]{2,1,0:T(2,128)S(1)}, f32[2,2,128]{2,1,0:T(2,128)S(1)}, u32[]{:S(2)}, u32[]{:S(2)}) collective-permute-start(f32[2,2,128]{2,1,0:T(2,128)S(1)} %get-tuple-element.43), channel_id=1, source_target_pairs={{1,0},{2,1},{3,2},{4,3},{5,4},{6,5},{7,6},{9,8},{10,9},{11,10},{12... | collective-permute-start | bytes 6152 | tf_op jit(solution)/shard_map/ppermute | solution.py:511
  11.7 5.2 %collective-permute-start.2 = (f32[2,2,128]{2,1,0:T(2,128)S(1)}, f32[2,2,128]{2,1,0:T(2,128)S(1)}, u32[]{:S(2)}, u32[]{:S(2)}) collective-permute-start(f32[2,2,128]{2,1,0:T(2,128)S(1)} %get-tuple-element.44), channel_id=1, source_target_pairs={{0,1},{1,2},{2,3},{3,4},{4,5},{5,6},{6,7},{8,9},{9,10},{10,11},{11... | collective-permute-start | bytes 6152 | tf_op jit(solution)/shard_map/ppermute | solution.py:507
  16.9 0.1 dynamic_slice.7
  17.0 0.1 broadcast_in_dim.2._.prec
  17.1 1.9 %copy-done.1 = f32[8,1,6,128,128]{4,3,2,1,0:T(8,128)S(1)} copy-done((f32[8,1,6,128,128]{4,3,2,1,0:T(8,128)S(1)}, f32[8,1,6,128,128]{4,3,2,1,0:T(8,128)}, u32[]{:S(2)}) %copy-start.1) | copy-done | bytes 3145752
  19.0 2.8 %copy-done.2 = bf16[8,512,1,6,128]{4,1,3,2,0:T(8,128)(2,1)S(1)} copy-done((bf16[8,512,1,6,128]{4,1,3,2,0:T(8,128)(2,1)S(1)}, bf16[8,512,1,6,128]{4,1,3,2,0:T(8,128)(2,1)}, u32[]{:S(2)}) %copy-start.2) | copy-done | bytes 6291480
  21.8 7.2 %before.1 = (f32[8,4,128,128]{3,2,1,0:T(8,128)S(1)}, f32[8,2,128,128]{3,2,1,0:T(8,128)S(1)}, f32[8,512,128]{2,1,0:T(8,128)S(1)}, bf16[8,6,128,512]{3,2,1,0:T(8,128)(2,1)S(1)}, bf16[8,512,512]{2,1,0:T(8,128)(2,1)S(1)}) custom-call(f32[8,6,128,128]{3,2,1,0:T(8,128)S(1)} %bitcast.18, f32[6,128]{1,0:T(8,128)S(1)} %get-tuple-element.48.diag, ...), custom_call_target="tpu_custom_call" | custom-call | bytes 12582912 | tf_op jit(solution)/shard_map/before/pallas_call | solution.py:210
  29.0 0.8 collective-permute-done.2.ctop
  29.7 3.2 %leaving.1 = (bf16[8,256,128]{2,1,0:T(8,128)(2,1)S(1)}, bf16[9,512,256]{2,1,0:T(8,128)(2,1)S(1)}) custom-call(s32[1]{0:T(128)} %bitcast.twin, bf16[2048,128]{1,0:T(8,128)(2,1)S(1)} %collective-permute-done.top, bf16[2048,128]{1,0:T(8,128)(2,1)S(1)} %collective-permute-done.1.bottom, f32[6,128]{1,0:T(8,128)S(1)} %get-tuple-element.48.diag, ...), custom_call_target="tpu_custom_call" | custom-call | bytes 1048576 | tf_op jit(solution)/shard_map/leaving/pallas_call | solution.py:267
  32.9 0.1 collective-permute-start.4
  33.0 1.5 %staying.1.mine = f32[8,256,128]{2,1,0:T(8,128)S(1)} custom-call(s32[1]{0:T(128)} %bitcast.twin, bf16[9,512,256]{2,1,0:T(8,128)(2,1)S(1)} %get-tuple-element.28.pairs, bf16[8,512,512]{2,1,0:T(8,128)(2,1)S(1)} %get-tuple-element.26.outward, f32[8,512,128]{2,1,0:T(8,128)S(1)} %get-tuple-element.27.start), custom_call_target="tpu_custom_call" | custom-call | bytes 1048576 | tf_op jit(solution)/shard_map/staying/pallas_call | solution.py:285
  34.5 0.4 collective-permute-done.4.got
  34.9 0.1 join.1
  35.0 20.7 %all_to_all.10.pieces = bf16[16,128,128]{2,1,0:T(8,128)(2,1)S(1)} all-to-all(bf16[16,128,128]{2,1,0:T(8,128)(2,1)S(1)} %bitcast.20), channel_id=1, replica_groups={{23,22,21,20,19,18,17,16,7,6,5,4,3,2,1,0},{31,30,29,28,27,26,25,24,15,1..., dimensions={0} | all-to-all | bytes 1048576 | tf_op jit(solution)/shard_map/all_to_all | solution.py:544
  55.7 0.1 scale.1
  55.8 18.8 %all_to_all.11.mine = bf16[16,128,128]{2,1,0:T(8,128)(2,1)S(1)} all-to-all(bf16[16,128,128]{2,1,0:T(8,128)(2,1)S(1)} %scale.1), channel_id=1, replica_groups=mesh['pair'=2,'twin'=2,'tile'=8] {'pair','tile'}, dimensions={0} | all-to-all | bytes 1048576 | tf_op jit(solution)/shard_map/all_to_all | solution.py:545
  74.6 1.6 %adjoint_own.1 = (f32[4,256,256]{2,1,0:T(8,128)S(1)}, f32[4,256,256]{2,1,0:T(8,128)S(1)}, bf16[9,256,256]{2,1,0:T(8,128)(2,1)S(1)}) custom-call(s32[1]{0:T(128)} %bitcast.twin, bf16[16,128,128]{2,1,0:T(8,128)(2,1)S(1)} %all_to_all.11.mine, bf16[8,6,128,512]{3,2,1,0:T(8,128)(2,1)S(1)} %get-tuple-element.30.turned), custom_call_target="tpu_custom_call" | custom-call | bytes 4194304 | tf_op jit(solution)/shard_map/adjoint_own/pallas_call | solution.py:357
  76.2 0.3 collective-permute-done.5.other
  76.5 0.9 adjoint_first.1
  77.4 1.3 %collective-permute-start.7 = (bf16[2048,128]{1,0:T(8,128)(2,1)S(1)}, bf16[2048,128]{1,0:T(8,128)(2,1)S(1)}, u32[]{:S(2)}, u32[]{:S(2)}) collective-permute-start(bf16[2048,128]{1,0:T(8,128)(2,1)S(1)} %get-tuple-element.34._), channel_id=1, source_target_pairs={{1,0},{2,1},{3,2},{4,3},{5,4},{6,5},{7,6},{9,8},{10,9},{11,10},{12... | collective-permute-start | bytes 1572872 | tf_op jit(solution)/shard_map/ppermute | solution.py:511
  78.7 0.9 adjoint_second.1
  79.6 4.6 %collective-permute-start.6 = (bf16[2048,128]{1,0:T(8,128)(2,1)S(1)}, bf16[2048,128]{1,0:T(8,128)(2,1)S(1)}, u32[]{:S(2)}, u32[]{:S(2)}) collective-permute-start(bf16[2048,128]{1,0:T(8,128)(2,1)S(1)} %get-tuple-element.35), channel_id=1, source_target_pairs={{0,1},{1,2},{2,3},{3,4},{4,5},{5,6},{6,7},{8,9},{9,10},{10,11},{11... | collective-permute-start | bytes 1572872 | tf_op jit(solution)/shard_map/ppermute | solution.py:507
  84.2 4.8 %inner.1 = (f32[8,4,128,128]{3,2,1,0:T(8,128)S(1)}, f32[8,2,128,128]{3,2,1,0:T(8,128)S(1)}, f32[8,6,128,128]{3,2,1,0:T(8,128)}, f32[2,8,128,128]{3,2,1,0:T(8,128)S(1)}) custom-call(s32[1]{0:T(128)} %bitcast.twin, bf16[9,256,256]{2,1,0:T(8,128)(2,1)S(1)} %get-tuple-element.36.own, bf16[9,256,256]{2,1,0:T(8,128)(2,1)S(1)} %get-tuple-element.32.pairs.got, ...), custom_call_target="tpu_custom_call" | custom-call | bytes 10485760 | tf_op jit(solution)/shard_map/inner/pallas_call | solution.py:460
  88.9 4.4 %collective-permute-done.7.message = bf16[2048,128]{1,0:T(8,128)(2,1)S(1)} collective-permute-done((bf16[2048,128]{1,0:T(8,128)(2,1)S(1)}, bf16[2048,128]{1,0:T(8,128)(2,1)S(1)}, u32[]{:S(2)}, u32[]{:S(2)}) %collective-permute-start.7) | collective-permute-done | bytes 524320 | tf_op jit(solution)/shard_map/ppermute | solution.py:511
  93.4 1.3 %finish.2._ = f32[8,6,128,128]{3,2,1,0:T(8,128)} custom-call(bf16[2048,128]{1,0:T(8,128)(2,1)S(1)} %collective-permute-done.7.message, f32[2,8,128,128]{3,2,1,0:T(8,128)S(1)} %get-tuple-element.39.mix, f32[8,4,128,128]{3,2,1,0:T(8,128)S(1)} %get-tuple-element.40.edges, ...), custom_call_target="tpu_custom_call", output_to_operand_aliasing={{}: (4, {})} | custom-call | bytes 2097152 | tf_op jit(solution)/shard_map/finish/pallas_call | solution.py:493
  94.7 8.9 %collective-permute-done.6.message = bf16[2048,128]{1,0:T(8,128)(2,1)S(1)} collective-permute-done((bf16[2048,128]{1,0:T(8,128)(2,1)S(1)}, bf16[2048,128]{1,0:T(8,128)(2,1)S(1)}, u32[]{:S(2)}, u32[]{:S(2)}) %collective-permute-start.6) | collective-permute-done | bytes 524320 | tf_op jit(solution)/shard_map/ppermute | solution.py:507
  103.6 1.3 %finish.3 = f32[8,6,128,128]{3,2,1,0:T(8,128)} custom-call(bf16[2048,128]{1,0:T(8,128)(2,1)S(1)} %collective-permute-done.6.message, f32[2,8,128,128]{3,2,1,0:T(8,128)S(1)} %get-tuple-element.39.mix, f32[8,4,128,128]{3,2,1,0:T(8,128)S(1)} %get-tuple-element.40.edges, ...), custom_call_target="tpu_custom_call", output_to_operand_aliasing={{}: (4, {})} | custom-call | bytes 2097152 | tf_op jit(solution)/shard_map/finish/pallas_call | solution.py:493
  (16 shorter events, 0.1 us)
Async XLA Ops:
  0.0 16.9 %copy-start = (f32[8,512]{1,0:T(8,128)S(1)}, f32[8,512]{1,0:T(8,128)}, u32[]{:S(2)}) copy-start(f32[8,512]{1,0:T(8,128)} %param.9) | copy-start | bytes 49156
  2.1 8.3 %copy-start.3 = (f32[1,6,128]{2,0,1:T(1,128)S(1)}, f32[1,6,128]{2,0,1:T(1,128)}, u32[]{:S(2)}) copy-start(f32[1,6,128]{2,0,1:T(1,128)} %param.6) | copy-start | bytes 9220
  2.1 8.3 %copy-start.4 = (f32[1,6,128]{2,0,1:T(1,128)S(1)}, f32[1,6,128]{2,0,1:T(1,128)}, u32[]{:S(2)}) copy-start(f32[1,6,128]{2,0,1:T(1,128)} %param.7) | copy-start | bytes 9220
  2.1 27.6 %collective-permute-start = (bf16[2048,128]{1,0:T(8,128)(2,1)}, bf16[2048,128]{1,0:T(8,128)(2,1)S(1)}, u32[]{:S(2)}, u32[]{:S(2)}) collective-permute-start(bf16[2048,128]{1,0:T(8,128)(2,1)} %pack.2._), channel_id=1, source_target_pairs={{0,1},{1,2},{2,3},{3,4},{4,5},{5,6},{6,7},{8,9},{9,10},{10,11},{11... | collective-permute-start | bytes 1572872 | tf_op jit(solution)/shard_map/ppermute | solution.py:507
  9.0 20.7 %collective-permute-start.1 = (bf16[2048,128]{1,0:T(8,128)(2,1)}, bf16[2048,128]{1,0:T(8,128)(2,1)S(1)}, u32[]{:S(2)}, u32[]{:S(2)}) collective-permute-start(bf16[2048,128]{1,0:T(8,128)(2,1)} %pack.3), channel_id=1, source_target_pairs={{1,0},{2,1},{3,2},{4,3},{5,4},{6,5},{7,6},{9,8},{10,9},{11,10},{12... | collective-permute-start | bytes 1572872 | tf_op jit(solution)/shard_map/ppermute | solution.py:511
  10.4 18.6 %collective-permute-start.3 = (f32[2,2,128]{2,1,0:T(2,128)S(1)}, f32[2,2,128]{2,1,0:T(2,128)S(1)}, u32[]{:S(2)}, u32[]{:S(2)}) collective-permute-start(f32[2,2,128]{2,1,0:T(2,128)S(1)} %get-tuple-element.43), channel_id=1, source_target_pairs={{1,0},{2,1},{3,2},{4,3},{5,4},{6,5},{7,6},{9,8},{10,9},{11,10},{12... | collective-permute-start | bytes 6152 | tf_op jit(solution)/shard_map/ppermute | solution.py:511
  11.7 18.0 %collective-permute-start.2 = (f32[2,2,128]{2,1,0:T(2,128)S(1)}, f32[2,2,128]{2,1,0:T(2,128)S(1)}, u32[]{:S(2)}, u32[]{:S(2)}) collective-permute-start(f32[2,2,128]{2,1,0:T(2,128)S(1)} %get-tuple-element.44), channel_id=1, source_target_pairs={{0,1},{1,2},{2,3},{3,4},{4,5},{5,6},{6,7},{8,9},{9,10},{10,11},{11... | collective-permute-start | bytes 6152 | tf_op jit(solution)/shard_map/ppermute | solution.py:507
  17.1 1.9 %copy-start.1 = (f32[8,1,6,128,128]{4,3,2,1,0:T(8,128)S(1)}, f32[8,1,6,128,128]{4,3,2,1,0:T(8,128)}, u32[]{:S(2)}) copy-start(f32[8,1,6,128,128]{4,3,2,1,0:T(8,128)} %_.1) | copy-start | bytes 9437188
  19.0 2.8 %copy-start.2 = (bf16[8,512,1,6,128]{4,1,3,2,0:T(8,128)(2,1)S(1)}, bf16[8,512,1,6,128]{4,1,3,2,0:T(8,128)(2,1)}, u32[]{:S(2)}) copy-start(bf16[8,512,1,6,128]{4,1,3,2,0:T(8,128)(2,1)} %param.8) | copy-start | bytes 18874372
  32.9 2.0 %collective-permute-start.4 = (bf16[8,256,128]{2,1,0:T(8,128)(2,1)S(1)}, bf16[8,256,128]{2,1,0:T(8,128)(2,1)S(1)}, u32[]{:S(2)}, u32[]{:S(2)}) collective-permute-start(bf16[8,256,128]{2,1,0:T(8,128)(2,1)S(1)} %get-tuple-element.29), channel_id=1, source_target_pairs={{0,8},{8,0},{1,9},{9,1},{2,10},{10,2},{3,11},{11,3},{4,12},{12,4},... | collective-permute-start | bytes 1572872 | tf_op jit(solution)/shard_map/ppermute | solution.py:515
  74.6 1.9 %collective-permute-start.5 = (bf16[16,128,128]{2,1,0:T(8,128)(2,1)S(1)}, bf16[16,128,128]{2,1,0:T(8,128)(2,1)S(1)}, u32[]{:S(2)}, u32[]{:S(2)}) collective-permute-start(bf16[16,128,128]{2,1,0:T(8,128)(2,1)S(1)} %all_to_all.11.mine), channel_id=1, source_target_pairs={{0,8},{8,0},{1,9},{9,1},{2,10},{10,2},{3,11},{11,3},{4,12},{12,4},... | collective-permute-start | bytes 1572872 | tf_op jit(solution)/shard_map/ppermute | solution.py:515
  77.4 15.9 %collective-permute-start.7 = (bf16[2048,128]{1,0:T(8,128)(2,1)S(1)}, bf16[2048,128]{1,0:T(8,128)(2,1)S(1)}, u32[]{:S(2)}, u32[]{:S(2)}) collective-permute-start(bf16[2048,128]{1,0:T(8,128)(2,1)S(1)} %get-tuple-element.34._), channel_id=1, source_target_pairs={{1,0},{2,1},{3,2},{4,3},{5,4},{6,5},{7,6},{9,8},{10,9},{11,10},{12... | collective-permute-start | bytes 1572872 | tf_op jit(solution)/shard_map/ppermute | solution.py:511
  79.6 24.0 %collective-permute-start.6 = (bf16[2048,128]{1,0:T(8,128)(2,1)S(1)}, bf16[2048,128]{1,0:T(8,128)(2,1)S(1)}, u32[]{:S(2)}, u32[]{:S(2)}) collective-permute-start(bf16[2048,128]{1,0:T(8,128)(2,1)S(1)} %get-tuple-element.35), channel_id=1, source_target_pairs={{0,1},{1,2},{2,3},{3,4},{4,5},{5,6},{6,7},{8,9},{9,10},{10,11},{11... | collective-permute-start | bytes 1572872 | tf_op jit(solution)/shard_map/ppermute | solution.py:507

commit v3 on v2

--- a/solution.py
+++ b/solution.py
@@ -313,7 +313,7 @@
     pairs[steps, :, width : 2 * width] = jnp.zeros((kept, width), pairs.dtype)
     for piece in range(groups):
         step, first = divmod(piece * share, kept)
-        value = source[groups - 1 - piece]
+        value = source[piece]
         pairs[step + 1, first : first + share, 0:width] = value
         pairs[step, first : first + share, width : 2 * width] = value
 
@@ -542,7 +542,7 @@
     both = join(staying(which, pairs, outward, data), swap_twins(gone)).reshape(groups, share, width)
     backwards = [list(reversed(range(groups)))]
     pieces = lax.all_to_all(both, others, 0, 0, axis_index_groups=backwards, tiled=True)
-    weighted = lax.all_to_all(scale(pieces, prec), others, 0, 0, tiled=True)
+    weighted = lax.all_to_all(scale(pieces, prec), others, 0, 0, axis_index_groups=backwards, tiled=True)
     other = swap_twins(weighted)
     tail, head, own = adjoint_own(which, weighted, turned)
     upper, head, got = adjoint_first(which, other, turned, head)

time: 106 us -> 106 us (level)
  waiting for transfers between devices: 14.7 us -> 15.9 us
    ppermute x3, waiting for transfers between devices: 9.63 us -> 10.8 us  [send_down(): lax.ppermute(tail, 'tile', [(i, i + 1) for i in range(lax.axis_size('tile...]
where the time goes in v3:
time: 106 us; the launch traced here: 105 us
  blocking collectives  38.5 us (36%)
  Pallas kernels  27 us (25%)
  starting transfers between devices  18.6 us (18%)
  waiting for transfers between devices  15.9 us (15%)
  local copies, waits for them, and re-layouts  4.88 us (5%)
    all_to_all x1, blocking collectives, body(): lax.all_to_all(both, others, 0, 0, axis_index_groups=backwards, tiled=True)  20.7 us
    all_to_all x1, blocking collectives, body(): lax.all_to_all(scale(pieces, prec), others, 0, 0, axis_index_groups=backw...  17.8 us
    ppermute x3, starting transfers between devices, send_down(): lax.ppermute(tail, 'tile', [(i, i + 1) for i in range(lax.axis_size('tile...  14.6 us
    ppermute x3, waiting for transfers between devices, send_down(): lax.ppermute(tail, 'tile', [(i, i + 1) for i in range(lax.axis_size('tile...  10.8 us
    pallas_call x1, Pallas kernels, before(): call(before_kernel, 'before', (f32(steps, 2 * HALO, cols, width), f32(ste...  7.19 us
    pallas_call x1, Pallas kernels, inner(): call(inner_kernel, 'inner', (f32(steps, 2 * HALO, cols, width), f32(steps...  4.76 us
    unnamed x13, local copies, waits for them, and re-layouts  4.71 us
    ppermute x3, waiting for transfers between devices, send_up(): lax.ppermute(head, 'tile', [(i + 1, i) for i in range(lax.axis_size('tile...  4.43 us
  transfers between devices with their start and end apart: 8, of which 5 were waited for; matrix products, arithmetic and copies ran while one was open for 0% of the time, Pallas kernels for 18%

profile of v3, /device:TPU:0, one launch (start us, length us, event | category | flops | bytes accessed | tf_op | source)
XLA Modules:
  0.0 105.1 jit_solution(8248127258404732677)
XLA Ops:
  0.0 2.1 %pack.2._ = bf16[2048,128]{1,0:T(8,128)(2,1)} custom-call(f32[8,6,128,128]{3,2,1,0:T(8,128)} %bitcast.16, f32[8,1,6,128,128]{4,3,2,1,0:T(8,128)} %_.1), custom_call_target="tpu_custom_call" | custom-call | bytes 3145728 | tf_op jit(solution)/shard_map/pack/pallas_call | solution.py:148
  2.1 0.0 copy-start.3
  2.1 4.9 %collective-permute-start = (bf16[2048,128]{1,0:T(8,128)(2,1)}, bf16[2048,128]{1,0:T(8,128)(2,1)S(1)}, u32[]{:S(2)}, u32[]{:S(2)}) collective-permute-start(bf16[2048,128]{1,0:T(8,128)(2,1)} %pack.2._), channel_id=1, source_target_pairs={{0,1},{1,2},{2,3},{3,4},{4,5},{5,6},{6,7},{8,9},{9,10},{10,11},{11... | collective-permute-start | bytes 1572872 | tf_op jit(solution)/shard_map/ppermute | solution.py:507
  7.0 2.0 %pack.3 = bf16[2048,128]{1,0:T(8,128)(2,1)} custom-call(f32[8,6,128,128]{3,2,1,0:T(8,128)} %bitcast.17, bf16[2048,128]{1,0:T(8,128)(2,1)} %pack.2._), custom_call_target="tpu_custom_call" | custom-call | bytes 3145728 | tf_op jit(solution)/shard_map/pack/pallas_call | solution.py:148
  9.0 1.3 %collective-permute-start.1 = (bf16[2048,128]{1,0:T(8,128)(2,1)}, bf16[2048,128]{1,0:T(8,128)(2,1)S(1)}, u32[]{:S(2)}, u32[]{:S(2)}) collective-permute-start(bf16[2048,128]{1,0:T(8,128)(2,1)} %pack.3), channel_id=1, source_target_pairs={{1,0},{2,1},{3,2},{4,3},{5,4},{6,5},{7,6},{9,8},{10,9},{11,10},{12... | collective-permute-start | bytes 1572872 | tf_op jit(solution)/shard_map/ppermute | solution.py:511
  10.4 1.3 %collective-permute-start.3 = (f32[2,2,128]{2,1,0:T(2,128)S(1)}, f32[2,2,128]{2,1,0:T(2,128)S(1)}, u32[]{:S(2)}, u32[]{:S(2)}) collective-permute-start(f32[2,2,128]{2,1,0:T(2,128)S(1)} %get-tuple-element.43), channel_id=1, source_target_pairs={{1,0},{2,1},{3,2},{4,3},{5,4},{6,5},{7,6},{9,8},{10,9},{11,10},{12... | collective-permute-start | bytes 6152 | tf_op jit(solution)/shard_map/ppermute | solution.py:511
  11.7 5.2 %collective-permute-start.2 = (f32[2,2,128]{2,1,0:T(2,128)S(1)}, f32[2,2,128]{2,1,0:T(2,128)S(1)}, u32[]{:S(2)}, u32[]{:S(2)}) collective-permute-start(f32[2,2,128]{2,1,0:T(2,128)S(1)} %get-tuple-element.44), channel_id=1, source_target_pairs={{0,1},{1,2},{2,3},{3,4},{4,5},{5,6},{6,7},{8,9},{9,10},{10,11},{11... | collective-permute-start | bytes 6152 | tf_op jit(solution)/shard_map/ppermute | solution.py:507
  16.9 0.1 dynamic_slice.7
  17.0 0.1 broadcast_in_dim.2._.prec
  17.1 1.9 %copy-done.1 = f32[8,1,6,128,128]{4,3,2,1,0:T(8,128)S(1)} copy-done((f32[8,1,6,128,128]{4,3,2,1,0:T(8,128)S(1)}, f32[8,1,6,128,128]{4,3,2,1,0:T(8,128)}, u32[]{:S(2)}) %copy-start.1) | copy-done | bytes 3145752
  19.0 2.8 %copy-done.2 = bf16[8,512,1,6,128]{4,1,3,2,0:T(8,128)(2,1)S(1)} copy-done((bf16[8,512,1,6,128]{4,1,3,2,0:T(8,128)(2,1)S(1)}, bf16[8,512,1,6,128]{4,1,3,2,0:T(8,128)(2,1)}, u32[]{:S(2)}) %copy-start.2) | copy-done | bytes 6291480
  21.8 7.2 %before.1 = (f32[8,4,128,128]{3,2,1,0:T(8,128)S(1)}, f32[8,2,128,128]{3,2,1,0:T(8,128)S(1)}, f32[8,512,128]{2,1,0:T(8,128)S(1)}, bf16[8,6,128,512]{3,2,1,0:T(8,128)(2,1)S(1)}, bf16[8,512,512]{2,1,0:T(8,128)(2,1)S(1)}) custom-call(f32[8,6,128,128]{3,2,1,0:T(8,128)S(1)} %bitcast.18, f32[6,128]{1,0:T(8,128)S(1)} %get-tuple-element.48.diag, ...), custom_call_target="tpu_custom_call" | custom-call | bytes 12582912 | tf_op jit(solution)/shard_map/before/pallas_call | solution.py:210
  29.0 0.8 collective-permute-done.2.ctop
  29.7 3.2 %leaving.1 = (bf16[8,256,128]{2,1,0:T(8,128)(2,1)S(1)}, bf16[9,512,256]{2,1,0:T(8,128)(2,1)S(1)}) custom-call(s32[1]{0:T(128)} %bitcast.twin, bf16[2048,128]{1,0:T(8,128)(2,1)S(1)} %collective-permute-done.top, bf16[2048,128]{1,0:T(8,128)(2,1)S(1)} %collective-permute-done.1.bottom, f32[6,128]{1,0:T(8,128)S(1)} %get-tuple-element.48.diag, ...), custom_call_target="tpu_custom_call" | custom-call | bytes 1048576 | tf_op jit(solution)/shard_map/leaving/pallas_call | solution.py:267
  32.9 0.1 collective-permute-start.4
  33.0 1.5 %staying.1.mine = f32[8,256,128]{2,1,0:T(8,128)S(1)} custom-call(s32[1]{0:T(128)} %bitcast.twin, bf16[9,512,256]{2,1,0:T(8,128)(2,1)S(1)} %get-tuple-element.28.pairs, bf16[8,512,512]{2,1,0:T(8,128)(2,1)S(1)} %get-tuple-element.26.outward, f32[8,512,128]{2,1,0:T(8,128)S(1)} %get-tuple-element.27.start), custom_call_target="tpu_custom_call" | custom-call | bytes 1048576 | tf_op jit(solution)/shard_map/staying/pallas_call | solution.py:285
  34.5 0.4 collective-permute-done.4.got
  34.9 0.1 join.1
  35.0 20.7 %all_to_all.10.pieces = bf16[16,128,128]{2,1,0:T(8,128)(2,1)S(1)} all-to-all(bf16[16,128,128]{2,1,0:T(8,128)(2,1)S(1)} %bitcast.20), channel_id=1, replica_groups={{23,22,21,20,19,18,17,16,7,6,5,4,3,2,1,0},{31,30,29,28,27,26,25,24,15,1..., dimensions={0} | all-to-all | bytes 1048576 | tf_op jit(solution)/shard_map/all_to_all | solution.py:544
  55.7 0.1 scale.1
  55.8 17.8 %all_to_all.11.mine = bf16[16,128,128]{2,1,0:T(8,128)(2,1)S(1)} all-to-all(bf16[16,128,128]{2,1,0:T(8,128)(2,1)S(1)} %scale.1), channel_id=1, replica_groups={{23,22,21,20,19,18,17,16,7,6,5,4,3,2,1,0},{31,30,29,28,27,26,25,24,15,1..., dimensions={0} | all-to-all | bytes 1048576 | tf_op jit(solution)/shard_map/all_to_all | solution.py:545
  73.6 1.6 %adjoint_own.1 = (f32[4,256,256]{2,1,0:T(8,128)S(1)}, f32[4,256,256]{2,1,0:T(8,128)S(1)}, bf16[9,256,256]{2,1,0:T(8,128)(2,1)S(1)}) custom-call(s32[1]{0:T(128)} %bitcast.twin, bf16[16,128,128]{2,1,0:T(8,128)(2,1)S(1)} %all_to_all.11.mine, bf16[8,6,128,512]{3,2,1,0:T(8,128)(2,1)S(1)} %get-tuple-element.30.turned), custom_call_target="tpu_custom_call" | custom-call | bytes 4194304 | tf_op jit(solution)/shard_map/adjoint_own/pallas_call | solution.py:357
  75.2 0.3 collective-permute-done.5.other
  75.5 0.9 adjoint_first.1
  76.4 1.3 %collective-permute-start.7 = (bf16[2048,128]{1,0:T(8,128)(2,1)S(1)}, bf16[2048,128]{1,0:T(8,128)(2,1)S(1)}, u32[]{:S(2)}, u32[]{:S(2)}) collective-permute-start(bf16[2048,128]{1,0:T(8,128)(2,1)S(1)} %get-tuple-element.34._), channel_id=1, source_target_pairs={{1,0},{2,1},{3,2},{4,3},{5,4},{6,5},{7,6},{9,8},{10,9},{11,10},{12... | collective-permute-start | bytes 1572872 | tf_op jit(solution)/shard_map/ppermute | solution.py:511
  77.7 0.9 adjoint_second.1
  78.6 4.6 %collective-permute-start.6 = (bf16[2048,128]{1,0:T(8,128)(2,1)S(1)}, bf16[2048,128]{1,0:T(8,128)(2,1)S(1)}, u32[]{:S(2)}, u32[]{:S(2)}) collective-permute-start(bf16[2048,128]{1,0:T(8,128)(2,1)S(1)} %get-tuple-element.35), channel_id=1, source_target_pairs={{0,1},{1,2},{2,3},{3,4},{4,5},{5,6},{6,7},{8,9},{9,10},{10,11},{11... | collective-permute-start | bytes 1572872 | tf_op jit(solution)/shard_map/ppermute | solution.py:507
  83.2 4.8 %inner.1 = (f32[8,4,128,128]{3,2,1,0:T(8,128)S(1)}, f32[8,2,128,128]{3,2,1,0:T(8,128)S(1)}, f32[8,6,128,128]{3,2,1,0:T(8,128)}, f32[2,8,128,128]{3,2,1,0:T(8,128)S(1)}) custom-call(s32[1]{0:T(128)} %bitcast.twin, bf16[9,256,256]{2,1,0:T(8,128)(2,1)S(1)} %get-tuple-element.36.own, bf16[9,256,256]{2,1,0:T(8,128)(2,1)S(1)} %get-tuple-element.32.pairs.got, ...), custom_call_target="tpu_custom_call" | custom-call | bytes 10485760 | tf_op jit(solution)/shard_map/inner/pallas_call | solution.py:460
  88.0 4.4 %collective-permute-done.7.message = bf16[2048,128]{1,0:T(8,128)(2,1)S(1)} collective-permute-done((bf16[2048,128]{1,0:T(8,128)(2,1)S(1)}, bf16[2048,128]{1,0:T(8,128)(2,1)S(1)}, u32[]{:S(2)}, u32[]{:S(2)}) %collective-permute-start.7) | collective-permute-done | bytes 524320 | tf_op jit(solution)/shard_map/ppermute | solution.py:511
  92.4 1.3 %finish.2._ = f32[8,6,128,128]{3,2,1,0:T(8,128)} custom-call(bf16[2048,128]{1,0:T(8,128)(2,1)S(1)} %collective-permute-done.7.message, f32[2,8,128,128]{3,2,1,0:T(8,128)S(1)} %get-tuple-element.39.mix, f32[8,4,128,128]{3,2,1,0:T(8,128)S(1)} %get-tuple-element.40.edges, ...), custom_call_target="tpu_custom_call", output_to_operand_aliasing={{}: (4, {})} | custom-call | bytes 2097152 | tf_op jit(solution)/shard_map/finish/pallas_call | solution.py:493
  93.7 10.0 %collective-permute-done.6.message = bf16[2048,128]{1,0:T(8,128)(2,1)S(1)} collective-permute-done((bf16[2048,128]{1,0:T(8,128)(2,1)S(1)}, bf16[2048,128]{1,0:T(8,128)(2,1)S(1)}, u32[]{:S(2)}, u32[]{:S(2)}) %collective-permute-start.6) | collective-permute-done | bytes 524320 | tf_op jit(solution)/shard_map/ppermute | solution.py:507
  103.8 1.3 %finish.3 = f32[8,6,128,128]{3,2,1,0:T(8,128)} custom-call(bf16[2048,128]{1,0:T(8,128)(2,1)S(1)} %collective-permute-done.6.message, f32[2,8,128,128]{3,2,1,0:T(8,128)S(1)} %get-tuple-element.39.mix, f32[8,4,128,128]{3,2,1,0:T(8,128)S(1)} %get-tuple-element.40.edges, ...), custom_call_target="tpu_custom_call", output_to_operand_aliasing={{}: (4, {})} | custom-call | bytes 2097152 | tf_op jit(solution)/shard_map/finish/pallas_call | solution.py:493
  (16 shorter events, 0.1 us)
Async XLA Ops:
  0.0 16.9 %copy-start = (f32[8,512]{1,0:T(8,128)S(1)}, f32[8,512]{1,0:T(8,128)}, u32[]{:S(2)}) copy-start(f32[8,512]{1,0:T(8,128)} %param.9) | copy-start | bytes 49156
  2.1 8.3 %copy-start.3 = (f32[1,6,128]{2,0,1:T(1,128)S(1)}, f32[1,6,128]{2,0,1:T(1,128)}, u32[]{:S(2)}) copy-start(f32[1,6,128]{2,0,1:T(1,128)} %param.6) | copy-start | bytes 9220
  2.1 8.3 %copy-start.4 = (f32[1,6,128]{2,0,1:T(1,128)S(1)}, f32[1,6,128]{2,0,1:T(1,128)}, u32[]{:S(2)}) copy-start(f32[1,6,128]{2,0,1:T(1,128)} %param.7) | copy-start | bytes 9220
  2.1 27.6 %collective-permute-start = (bf16[2048,128]{1,0:T(8,128)(2,1)}, bf16[2048,128]{1,0:T(8,128)(2,1)S(1)}, u32[]{:S(2)}, u32[]{:S(2)}) collective-permute-start(bf16[2048,128]{1,0:T(8,128)(2,1)} %pack.2._), channel_id=1, source_target_pairs={{0,1},{1,2},{2,3},{3,4},{4,5},{5,6},{6,7},{8,9},{9,10},{10,11},{11... | collective-permute-start | bytes 1572872 | tf_op jit(solution)/shard_map/ppermute | solution.py:507
  9.0 20.7 %collective-permute-start.1 = (bf16[2048,128]{1,0:T(8,128)(2,1)}, bf16[2048,128]{1,0:T(8,128)(2,1)S(1)}, u32[]{:S(2)}, u32[]{:S(2)}) collective-permute-start(bf16[2048,128]{1,0:T(8,128)(2,1)} %pack.3), channel_id=1, source_target_pairs={{1,0},{2,1},{3,2},{4,3},{5,4},{6,5},{7,6},{9,8},{10,9},{11,10},{12... | collective-permute-start | bytes 1572872 | tf_op jit(solution)/shard_map/ppermute | solution.py:511
  10.4 18.6 %collective-permute-start.3 = (f32[2,2,128]{2,1,0:T(2,128)S(1)}, f32[2,2,128]{2,1,0:T(2,128)S(1)}, u32[]{:S(2)}, u32[]{:S(2)}) collective-permute-start(f32[2,2,128]{2,1,0:T(2,128)S(1)} %get-tuple-element.43), channel_id=1, source_target_pairs={{1,0},{2,1},{3,2},{4,3},{5,4},{6,5},{7,6},{9,8},{10,9},{11,10},{12... | collective-permute-start | bytes 6152 | tf_op jit(solution)/shard_map/ppermute | solution.py:511
  11.7 18.0 %collective-permute-start.2 = (f32[2,2,128]{2,1,0:T(2,128)S(1)}, f32[2,2,128]{2,1,0:T(2,128)S(1)}, u32[]{:S(2)}, u32[]{:S(2)}) collective-permute-start(f32[2,2,128]{2,1,0:T(2,128)S(1)} %get-tuple-element.44), channel_id=1, source_target_pairs={{0,1},{1,2},{2,3},{3,4},{4,5},{5,6},{6,7},{8,9},{9,10},{10,11},{11... | collective-permute-start | bytes 6152 | tf_op jit(solution)/shard_map/ppermute | solution.py:507
  17.1 1.9 %copy-start.1 = (f32[8,1,6,128,128]{4,3,2,1,0:T(8,128)S(1)}, f32[8,1,6,128,128]{4,3,2,1,0:T(8,128)}, u32[]{:S(2)}) copy-start(f32[8,1,6,128,128]{4,3,2,1,0:T(8,128)} %_.1) | copy-start | bytes 9437188
  19.0 2.8 %copy-start.2 = (bf16[8,512,1,6,128]{4,1,3,2,0:T(8,128)(2,1)S(1)}, bf16[8,512,1,6,128]{4,1,3,2,0:T(8,128)(2,1)}, u32[]{:S(2)}) copy-start(bf16[8,512,1,6,128]{4,1,3,2,0:T(8,128)(2,1)} %param.8) | copy-start | bytes 18874372
  32.9 2.0 %collective-permute-start.4 = (bf16[8,256,128]{2,1,0:T(8,128)(2,1)S(1)}, bf16[8,256,128]{2,1,0:T(8,128)(2,1)S(1)}, u32[]{:S(2)}, u32[]{:S(2)}) collective-permute-start(bf16[8,256,128]{2,1,0:T(8,128)(2,1)S(1)} %get-tuple-element.29), channel_id=1, source_target_pairs={{0,8},{8,0},{1,9},{9,1},{2,10},{10,2},{3,11},{11,3},{4,12},{12,4},... | collective-permute-start | bytes 1572872 | tf_op jit(solution)/shard_map/ppermute | solution.py:515
  73.6 1.9 %collective-permute-start.5 = (bf16[16,128,128]{2,1,0:T(8,128)(2,1)S(1)}, bf16[16,128,128]{2,1,0:T(8,128)(2,1)S(1)}, u32[]{:S(2)}, u32[]{:S(2)}) collective-permute-start(bf16[16,128,128]{2,1,0:T(8,128)(2,1)S(1)} %all_to_all.11.mine), channel_id=1, source_target_pairs={{0,8},{8,0},{1,9},{9,1},{2,10},{10,2},{3,11},{11,3},{4,12},{12,4},... | collective-permute-start | bytes 1572872 | tf_op jit(solution)/shard_map/ppermute | solution.py:515
  76.4 15.9 %collective-permute-start.7 = (bf16[2048,128]{1,0:T(8,128)(2,1)S(1)}, bf16[2048,128]{1,0:T(8,128)(2,1)S(1)}, u32[]{:S(2)}, u32[]{:S(2)}) collective-permute-start(bf16[2048,128]{1,0:T(8,128)(2,1)S(1)} %get-tuple-element.34._), channel_id=1, source_target_pairs={{1,0},{2,1},{3,2},{4,3},{5,4},{6,5},{7,6},{9,8},{10,9},{11,10},{12... | collective-permute-start | bytes 1572872 | tf_op jit(solution)/shard_map/ppermute | solution.py:511
  78.6 25.2 %collective-permute-start.6 = (bf16[2048,128]{1,0:T(8,128)(2,1)S(1)}, bf16[2048,128]{1,0:T(8,128)(2,1)S(1)}, u32[]{:S(2)}, u32[]{:S(2)}) collective-permute-start(bf16[2048,128]{1,0:T(8,128)(2,1)S(1)} %get-tuple-element.35), channel_id=1, source_target_pairs={{0,1},{1,2},{2,3},{3,4},{4,5},{5,6},{6,7},{8,9},{9,10},{10,11},{11... | collective-permute-start | bytes 1572872 | tf_op jit(solution)/shard_map/ppermute | solution.py:507
